TPU v7x, 32 devices: a whole 2x2x4 slice. The times are simulated.
32 devices in a mesh: dp: 4 (over y, core), seq: 8 (over z, x).
Axes of the slice: x: 2, y: 2, z: 4, core: 2. Of those that a mesh axis runs over, the one named last changes fastest.
Arguments:
- inputs: bfloat16 [2, 65536, 2048], P(None, 'seq', 'dp'), may hold values from -6 to 6
- cotangent: bfloat16 [2, 65536, 2048], P(None, 'seq', 'dp'), may hold values from -6 to 6
- kernel: bfloat16 [65536, 2048], P('seq', 'dp'), may hold values from -6 to 6
- factor_one: bfloat16 [256, 256], replicated, may hold values from -0.375 to 0.375
- factor_two: bfloat16 [256, 256], replicated, may hold values from -0.375 to 0.375
Outputs:
- grad_inputs: bfloat16 [2, 65536, 2048], P(None, 'seq', 'dp')
- grad_kernel: bfloat16 [65536, 2048], P('seq', 'dp')
- grad_factor_one: float32 [256, 256], replicated
- grad_factor_two: float32 [256, 256], replicated
All inputs are finite; a program needn't handle non-finite values.
Results may differ from a plain program's by a relative error of at most 0.0085.
Values may be sent and summed in bfloat16 or wider, within the bound.
No kernel may reach another device: no remote copies, remote signals or barrier semaphores. Data moves between devices by JAX's collectives and lax.ppermute only.
A program may use at most 256 MiB of HBM per device.

v0:
```python
import math

import jax
import jax.numpy as jnp
from jax import lax
from jax.sharding import PartitionSpec as P


def within_blocks(factor, values):
    return jnp.einsum("cb,nabh->nach", factor, values, preferred_element_type=jnp.float32)


def within_blocks_back(factor, values):
    return jnp.einsum("cb,nach->nabh", factor, values, preferred_element_type=jnp.float32)


def across_blocks(factor, values):
    return jnp.einsum("ea,nach->nech", factor, values, preferred_element_type=jnp.float32)


def across_blocks_back(factor, values):
    return jnp.einsum("ea,nech->nach", factor, values, preferred_element_type=jnp.float32)


def pair_product(left, right):
    return jnp.einsum("nech,nach->ea", left, right, preferred_element_type=jnp.float32)


def on_device(inputs, cotangent, kernel, factor_one, factor_two):
    batch_count = inputs.shape[0]
    row_count = inputs.shape[1]
    channels = inputs.shape[2]
    block_size = factor_one.shape[0]
    block_count = factor_two.shape[0]
    local_blocks = row_count // block_size
    inputs_cube = inputs.reshape(batch_count, local_blocks, block_size, channels)
    grads_cube = cotangent.reshape(batch_count, local_blocks, block_size, channels)
    kernel_cube = kernel.reshape(local_blocks, block_size, channels)
    within_mix = within_blocks(factor_one, inputs_cube).astype(jnp.bfloat16)
    within_spread = lax.all_to_all(within_mix, "seq", split_axis=2, concat_axis=1, tiled=True)
    spectrum = across_blocks(factor_two, within_spread).astype(jnp.bfloat16)
    grad_within = within_blocks(factor_one, grads_cube).astype(jnp.bfloat16)
    grad_spread = lax.all_to_all(grad_within, "seq", split_axis=2, concat_axis=1, tiled=True)
    grad_spectrum = across_blocks(factor_two, grad_spread).astype(jnp.bfloat16)
    kernel_spread = lax.all_to_all(
        kernel_cube, "seq", split_axis=1, concat_axis=0, tiled=True
    ).astype(jnp.float32)[None]
    weighted = (kernel_spread * spectrum.astype(jnp.float32)).astype(jnp.bfloat16)
    grad_weighted = (kernel_spread * grad_spectrum.astype(jnp.float32)).astype(jnp.bfloat16)
    kernel_terms = jnp.sum(grad_spectrum.astype(jnp.float32) * spectrum.astype(jnp.float32), axis=0)
    returned_spread = across_blocks_back(factor_two, weighted).astype(jnp.bfloat16)
    grad_returned_spread = across_blocks_back(factor_two, grad_weighted).astype(jnp.bfloat16)
    second_terms = pair_product(weighted, grad_spread) + pair_product(grad_weighted, within_spread)
    returned, grad_returned = (
        lax.all_to_all(returned_spread, "seq", split_axis=1, concat_axis=2, tiled=True),
        lax.all_to_all(grad_returned_spread, "seq", split_axis=1, concat_axis=2, tiled=True),
    )
    grad_inputs = within_blocks_back(factor_one, grad_returned).astype(jnp.bfloat16)
    first_terms = jnp.einsum(
        "nach,nabh->cb", returned, grads_cube, preferred_element_type=jnp.float32
    )
    first_terms = first_terms + jnp.einsum(
        "nach,nabh->cb", grad_returned, inputs_cube, preferred_element_type=jnp.float32
    )
    first_total, second_total = lax.psum((first_terms, second_terms), ("dp", "seq"))
    kernel_half = kernel_terms.astype(jnp.bfloat16)
    kernel_half = lax.all_to_all(kernel_half, "seq", split_axis=0, concat_axis=1, tiled=True)
    grad_kernel = kernel_half.reshape(row_count, channels)
    full_width = channels * lax.axis_size("dp")
    scale_first = 1.0 / math.sqrt(batch_count * block_count * full_width)
    scale_second = 1.0 / math.sqrt(batch_count * block_size * full_width)
    return (
        grad_inputs.reshape(batch_count, row_count, channels),
        grad_kernel,
        first_total * scale_first,
        second_total * scale_second,
    )


def solution(mesh):
    return jax.shard_map(
        on_device,
        mesh=mesh,
        in_specs=(P(None, "seq", "dp"), P(None, "seq", "dp"), P("seq", "dp"), P(), P()),
        out_specs=(P(None, "seq", "dp"), P("seq", "dp"), P(), P()),
        check_vma=False,
    )
```

profile of v0, /device:TPU:3, one launch (start us, length us, event | category | flops | bytes accessed | tf_op | source)
XLA Modules:
  0.0 2153.1 jit_solution(10406760720790027508)
XLA Ops:
  36.5 28.1 %copy.141 = bf16[2,32,256,512]{3,1,0,2:T(8,128)(2,1)} copy(bf16[2,32,256,512]{2,3,1,0:T(8,128)(2,1)} %convert_bitcast_fusion.2) | data formatting | bytes 33554432 | tf_op jit(solution)/shard_map/convert_element_type | solution.py:39
  64.6 142.4 %all-to-all-done = bf16[32,256,512]{2,0,1:T(8,128)(2,1)} async-done(((bf16[32,256,512]{2,0,1:T(8,128)(2,1)}), bf16[32,256,512]{2,0,1:T(8,128)(2,1)}, u32[]{:S(2)}, u32[]{:S(2)}) %all-to-all-start) | async-done | bytes 8388640 | tf_op jit(solution)/shard_map/all_to_all | solution.py:45
  224.6 28.1 %copy.132 = bf16[2,32,256,512]{3,1,0,2:T(8,128)(2,1)} copy(bf16[2,32,256,512]{2,3,1,0:T(8,128)(2,1)} %convert_bitcast_fusion.4) | data formatting | bytes 33554432 | tf_op jit(solution)/shard_map/convert_element_type | solution.py:42
  252.7 321.9 %all-to-all-done.3 = bf16[2,32,256,512]{3,1,0,2:T(8,128)(2,1)} async-done(((bf16[2,32,256,512]{3,1,0,2:T(8,128)(2,1)}), bf16[2,32,256,512]{3,1,0,2:T(8,128)(2,1)}, u32[]{:S(2)}, u32[]{:S(2)}) %all-to-all-start.3) | async-done | bytes 16777248 | tf_op jit(solution)/shard_map/all_to_all | solution.py:40
  616.3 19.2 copy.130
  635.5 18.5 copy.143
  654.0 287.6 %all-to-all-done.1 = bf16[2,32,256,512]{3,1,0,2:T(8,128)(2,1)} async-done(((bf16[2,32,256,512]{3,1,0,2:T(8,128)(2,1)}), bf16[2,32,256,512]{3,1,0,2:T(8,128)(2,1)}, u32[]{:S(2)}, u32[]{:S(2)}) %all-to-all-start.1) | async-done | bytes 16777248 | tf_op jit(solution)/shard_map/all_to_all | solution.py:43
  941.7 18.5 copy.134
  960.1 53.3 %fusion.18 = bf16[2,32,512,256]{3,2,1,0:T(8,128)(2,1)} fusion(bf16[2,256,32,512]{3,2,1,0:T(8,128)(2,1)} %bitcast.102, bf16[256,256]{1,0:T(8,128)(2,1)S(1)} %copy-done), kind=kOutput, calls=%fused_computation.27 | convolution fusion | flops 4303355904 | bytes 33685504 | tf_op jit(solution)/shard_map/ea,nach->nech/dot_general | solution.py:18
  1013.5 37.0 %fusion.1 = (bf16[2,256,32,512]{1,3,2,0:T(8,128)(2,1)}, bf16[2,256,32,512]{1,3,2,0:T(8,128)(2,1)}, bf16[256,32,512]{0,2,1:T(8,128)(2,1)}) fusion(f32[256,32,512]{0,2,1:T(8,128)} %copy.130, bf16[2,32,512,256]{3,2,1,0:T(8,128)(2,1)} %fusion.18, bf16[256,256]{1,0:T(8,128)(2,1)S(1)} %copy-done, bf16[2,256,32,512]{3,2,1,0:T(8,128)(2,1)} %bitcast.104), kind=kOutput, calls=%fused_computation.3 | convolution fusion | flops 4366270464 | bytes 92405760 | tf_op jit(solution)/shard_map/ea,nach->nech/dot_general | solution.py:18
  1050.4 14.7 copy.145
  1082.6 28.1 %copy.147 = bf16[2,256,32,512]{3,2,0,1:T(8,128)(2,1)} copy(bf16[2,256,32,512]{1,3,2,0:T(8,128)(2,1)} %convert_bitcast_fusion.1) | data formatting | bytes 33554432 | tf_op jit(solution)/shard_map/convert_element_type | solution.py:51
  1110.7 142.4 %all-to-all-done.4 = bf16[256,32,512]{2,1,0:T(8,128)(2,1)} async-done(((bf16[256,32,512]{2,1,0:T(8,128)(2,1)}), bf16[256,32,512]{2,1,0:T(8,128)(2,1)}, u32[]{:S(2)}, u32[]{:S(2)}) %all-to-all-start.4) | async-done | bytes 8388640 | tf_op jit(solution)/shard_map/all_to_all | solution.py:67
  1270.7 28.1 %copy.136 = bf16[2,256,32,512]{3,2,0,1:T(8,128)(2,1)} copy(bf16[2,256,32,512]{1,3,2,0:T(8,128)(2,1)} %convert_bitcast_fusion.3) | data formatting | bytes 33554432 | tf_op jit(solution)/shard_map/convert_element_type | solution.py:52
  1298.8 321.9 %all-to-all-done.5 = bf16[2,256,32,512]{3,2,0,1:T(8,128)(2,1)} async-done(((bf16[2,256,32,512]{3,2,0,1:T(8,128)(2,1)}), bf16[2,256,32,512]{3,2,0,1:T(8,128)(2,1)}, u32[]{:S(2)}, u32[]{:S(2)}) %all-to-all-start.5) | async-done | bytes 16777248 | tf_op jit(solution)/shard_map/all_to_all | solution.py:55
  1626.5 31.6 %fusion.32 = f32[256,256]{1,0:T(8,128)S(1)} fusion(bf16[2,256,32,512]{3,2,1,0:T(8,128)(2,1)} %bitcast.103, bf16[2,256,32,512]{1,3,2,0:T(8,128)(2,1)} %get-tuple-element.6), kind=kOutput, calls=%fused_computation.31 | convolution fusion | flops 4294967296 | bytes 33816576 | tf_op jit(solution)/shard_map/nech,nach->ea/dot_general | solution.py:26
  1658.1 32.6 %fusion.42 = f32[256,256]{1,0:T(8,128)} fusion(f32[256,256]{1,0:T(8,128)S(1)} %fusion.32, bf16[2,256,32,512]{3,2,1,0:T(8,128)(2,1)} %bitcast.105, bf16[2,256,32,512]{1,3,2,0:T(8,128)(2,1)} %get-tuple-element.7), kind=kOutput, calls=%fused_computation.33 | convolution fusion | flops 4295032832 | bytes 34078720 | tf_op jit(solution)/shard_map/nech,nach->ea/dot_general | solution.py:26
  1699.1 14.2 copy.149
  1713.3 12.9 fusion.24
  1726.2 261.5 %all-to-all-done.2 = bf16[2,256,32,512]{3,2,0,1:T(8,128)(2,1)} async-done(((bf16[2,256,32,512]{3,2,0,1:T(8,128)(2,1)}), bf16[2,256,32,512]{3,2,0,1:T(8,128)(2,1)}, u32[]{:S(2)}, u32[]{:S(2)}) %all-to-all-start.2) | async-done | bytes 16777248 | tf_op jit(solution)/shard_map/all_to_all | solution.py:56
  1987.7 14.1 copy.138
  2001.9 13.7 fusion.47
  2015.6 14.6 convolution_convert_fusion
  2030.2 113.7 %all-reduce.3.cloned.1.call-done = (f32[256,256]{1,0:T(8,128)}, f32[256,256]{1,0:T(8,128)}) async-done(((f32[256,256]{1,0:T(8,128)}, f32[256,256]{1,0:T(8,128)}), (f32[256,256]{1,0:T(8,128)}, f32[256,256]{1,0:T(8,128)})) %all-reduce.3.cloned.1.call-update) | async-done | bytes 524304 | tf_op jit(solution)/shard_map/psum | solution.py:65
  (24 shorter events, 139.8 us)
Async XLA Ops:
  7.2 953.0 %copy-start = (bf16[256,256]{1,0:T(8,128)(2,1)S(1)}, bf16[256,256]{1,0:T(8,128)(2,1)}, u32[]{:S(2)}) copy-start(bf16[256,256]{1,0:T(8,128)(2,1)} %param.9) | copy-start | bytes 393220
  7.2 17.4 copy-start.1
  18.8 188.2 %all-to-all-start = ((bf16[32,256,512]{2,0,1:T(8,128)(2,1)}), bf16[32,256,512]{2,0,1:T(8,128)(2,1)}, u32[]{:S(2)}, u32[]{:S(2)}) async-start(bf16[32,256,512]{2,0,1:T(8,128)(2,1)} %copy.127), calls=%async_computation | async-start | bytes 16777216 | tf_op jit(solution)/shard_map/all_to_all | solution.py:45
  206.9 367.7 %all-to-all-start.3 = ((bf16[2,32,256,512]{3,1,0,2:T(8,128)(2,1)}), bf16[2,32,256,512]{3,1,0,2:T(8,128)(2,1)}, u32[]{:S(2)}, u32[]{:S(2)}) async-start(bf16[2,32,256,512]{3,1,0,2:T(8,128)(2,1)} %copy.141), calls=%async_computation.3 | async-start | bytes 33554432 | tf_op jit(solution)/shard_map/all_to_all | solution.py:40
  574.6 367.0 %all-to-all-start.1 = ((bf16[2,32,256,512]{3,1,0,2:T(8,128)(2,1)}), bf16[2,32,256,512]{3,1,0,2:T(8,128)(2,1)}, u32[]{:S(2)}, u32[]{:S(2)}) async-start(bf16[2,32,256,512]{3,1,0,2:T(8,128)(2,1)} %copy.132), calls=%async_computation.1 | async-start | bytes 33554432 | tf_op jit(solution)/shard_map/all_to_all | solution.py:43
  1065.1 187.9 %all-to-all-start.4 = ((bf16[256,32,512]{2,1,0:T(8,128)(2,1)}), bf16[256,32,512]{2,1,0:T(8,128)(2,1)}, u32[]{:S(2)}, u32[]{:S(2)}) async-start(bf16[256,32,512]{2,1,0:T(8,128)(2,1)} %copy.145), calls=%async_computation.4 | async-start | bytes 16777216 | tf_op jit(solution)/shard_map/all_to_all | solution.py:67
  1253.0 367.6 %all-to-all-start.5 = ((bf16[2,256,32,512]{3,2,0,1:T(8,128)(2,1)}), bf16[2,256,32,512]{3,2,0,1:T(8,128)(2,1)}, u32[]{:S(2)}, u32[]{:S(2)}) async-start(bf16[2,256,32,512]{3,2,0,1:T(8,128)(2,1)} %copy.147), calls=%async_computation.5 | async-start | bytes 33554432 | tf_op jit(solution)/shard_map/all_to_all | solution.py:55
  1620.7 367.1 %all-to-all-start.2 = ((bf16[2,256,32,512]{3,2,0,1:T(8,128)(2,1)}), bf16[2,256,32,512]{3,2,0,1:T(8,128)(2,1)}, u32[]{:S(2)}, u32[]{:S(2)}) async-start(bf16[2,256,32,512]{3,2,0,1:T(8,128)(2,1)} %copy.136), calls=%async_computation.2 | async-start | bytes 33554432 | tf_op jit(solution)/shard_map/all_to_all | solution.py:56
  1626.4 517.5 %all-reduce.3.cloned.1.call-start = ((), (), s32[]{:S(2)}) async-start(), calls=%async_computation.6 | async-start | bytes 1048576 | tf_op jit(solution)/shard_map/psum | solution.py:65
  2001.9 13.7 copy-start.2
Sparse Core Ops, SparseCore 0:
  2015.7 128.1 all-reduce.2
where the time goes:
time: 2170 us; the launch traced here: 2150 us
  waiting for transfers between devices  1590 us (73%)
  local copies, waits for them, and re-layouts  255 us (12%)
  matrix products  243 us (11%)
  starting transfers between devices  34.5 us (2%)
    all_to_all x1, waiting for transfers between devices, on_device(): lax.all_to_all(within_mix, 'seq', split_axis=2, concat_axis=1, tiled=True)  322 us
    all_to_all x1, waiting for transfers between devices, on_device(): lax.all_to_all(returned_spread, 'seq', split_axis=1, concat_axis=2, tiled...  322 us
    all_to_all x1, waiting for transfers between devices, on_device(): lax.all_to_all(grad_within, 'seq', split_axis=2, concat_axis=1, tiled=True)  288 us
    all_to_all x1, waiting for transfers between devices, on_device(): lax.all_to_all(grad_returned_spread, 'seq', split_axis=1, concat_axis=2,...  262 us
    all_to_all x1, waiting for transfers between devices, on_device(): lax.all_to_all(kernel_cube, 'seq', split_axis=1, concat_axis=0, tiled=True)  142 us
    all_to_all x1, waiting for transfers between devices, on_device(): lax.all_to_all(kernel_half, 'seq', split_axis=0, concat_axis=1, tiled=True)  142 us
    psum x1, waiting for transfers between devices, on_device(): lax.psum((first_terms, second_terms), ('dp', 'seq'))  114 us
    dot_general x2, matrix products, across_blocks(): jnp.einsum('ea,nach->nech', factor, values, preferred_element_type=jnp.fl...  90.3 us
  transfers between devices with their start and end apart: 7, of which 7 were waited for; matrix products, arithmetic and copies ran while one was open for 16% of the time, Pallas kernels for 0%

commit v1 on v0

v1 whole, which is shorter than its diff:
```python
import functools
import math

import jax
import jax.numpy as jnp
from jax import lax
from jax.experimental import pallas as pl
from jax.experimental.pallas import tpu as pltpu
from jax.sharding import PartitionSpec as P

WINDOW = 6
VMEM_BYTES = 60 * 1024 * 1024
LANES = 128
ROWS = 16


def matmul(left, right):
    return jnp.dot(left, right, preferred_element_type=jnp.float32)


def matmul_rows(left, right):
    return lax.dot_general(left, right, (((0,), (0,)), ((), ())), preferred_element_type=jnp.float32)


def matmul_columns(left, right):
    return lax.dot_general(left, right, (((1,), (1,)), ((), ())), preferred_element_type=jnp.float32)


def leave_kernel(group, me_ref, values_ref, *refs):
    outs, held = refs[:-1], refs[-1]
    mine = lax.rem(me_ref[0], group)
    turned = jnp.stack([values_ref[0, i].T for i in range(values_ref.shape[1])])
    held[...] = jnp.swapaxes(turned, 0, 1).reshape(held.shape)
    for j, out in enumerate(outs):
        out[...] = held[mine ^ j]


def leave(values, place, me, lane_block, group):
    _, blocks, width, channels = values.shape
    lanes = min(LANES, channels)
    own = lanes // group
    rows = math.gcd(blocks, ROWS)
    spec = pl.BlockSpec((own, rows, width), lambda i, me: (0, i, 0))
    return pl.pallas_call(
        functools.partial(leave_kernel, group),
        grid_spec=pltpu.PrefetchScalarGridSpec(
            num_scalar_prefetch=1,
            grid=(blocks // rows,),
            in_specs=[
                pl.BlockSpec((1, rows, width, lanes), lambda i, me: (place, i, 0, (me[0] // group) ^ lane_block))
            ],
            out_specs=[spec] * group,
            scratch_shapes=[pltpu.VMEM((group, own, rows, width), values.dtype)],
        ),
        out_shape=[jax.ShapeDtypeStruct((own, blocks, width), values.dtype)] * group,
        compiler_params=pltpu.CompilerParams(vmem_limit_bytes=VMEM_BYTES),
        cost_estimate=pl.CostEstimate(
            flops=0, bytes_accessed=4 * blocks * width * lanes, transcendentals=0
        ),
    )(me, values)


def arrive_kernel(group, me_ref, *refs):
    pieces, out_ref, held = refs[:group], refs[-2], refs[-1]
    own, blocks, width = pieces[0].shape
    mine = lax.rem(me_ref[0], group)
    for j, piece in enumerate(pieces):
        held[mine ^ j] = piece[...]
    turned = jnp.swapaxes(held[...].reshape(group * own, blocks, width), 0, 1)
    for i in range(blocks):
        out_ref[0, i] = turned[i].T


def arrive(pieces, me, lane_block, place, count, channels, onto):
    group = len(pieces)
    own, blocks, width = pieces[0].shape
    lanes = own * group
    rows = math.gcd(blocks, ROWS)
    spec = pl.BlockSpec((own, rows, width), lambda i, me: (0, i, 0))
    aliased = onto is not None
    return pl.pallas_call(
        functools.partial(arrive_kernel, group),
        grid_spec=pltpu.PrefetchScalarGridSpec(
            num_scalar_prefetch=1,
            grid=(blocks // rows,),
            in_specs=[spec] * group + ([pl.BlockSpec(memory_space=pl.ANY)] if aliased else []),
            out_specs=pl.BlockSpec(
                (1, rows, width, lanes), lambda i, me: (place, i, 0, (me[0] // group) ^ lane_block)
            ),
            scratch_shapes=[pltpu.VMEM((group, own, rows, width), pieces[0].dtype)],
        ),
        out_shape=jax.ShapeDtypeStruct((count, blocks, width, channels), pieces[0].dtype),
        input_output_aliases={group + 1: 0} if aliased else {},
        compiler_params=pltpu.CompilerParams(vmem_limit_bytes=VMEM_BYTES),
        cost_estimate=pl.CostEstimate(
            flops=0, bytes_accessed=4 * blocks * width * lanes, transcendentals=0
        ),
    )(me, *pieces, *((onto,) if aliased else ()))


def mix_kernel(parts, has_previous, is_last, *refs):
    refs = list(refs)
    take = lambda count: [refs.pop(0) for _ in range(count)]
    x_refs, y_refs, k_refs = take(parts), take(parts), take(parts)
    previous_ref = take(1)[0] if has_previous else None
    one_ref, one_t_ref, two_ref, two_t_ref = take(4)
    grad_refs = take(parts)
    kernel_refs = take(parts if is_last else 1)
    first_ref, second_ref = refs
    channel_count, part_rows, width = x_refs[0].shape

    @pl.when(pl.program_id(0) == 0)
    def _():
        first_ref[...] = jnp.zeros_like(first_ref)
        second_ref[...] = jnp.zeros_like(second_ref)

    def whole(group, channel):
        return jnp.concatenate([r[channel] for r in group], axis=0)

    def spread(group, channel, values):
        for part, ref in enumerate(group):
            ref[channel] = values[part * part_rows : (part + 1) * part_rows]

    one, one_t, two, two_t = one_ref[...], one_t_ref[...], two_ref[...], two_t_ref[...]
    first_sum = None
    second_sum = None
    for channel in range(channel_count):
        x, y = whole(x_refs, channel), whole(y_refs, channel)
        k = whole(k_refs, channel).astype(jnp.float32)
        a = matmul(x, one_t).astype(jnp.bfloat16)
        g = matmul(y, one_t).astype(jnp.bfloat16)
        s = matmul(two, a).astype(jnp.bfloat16).astype(jnp.float32)
        h = matmul(two, g).astype(jnp.bfloat16).astype(jnp.float32)
        z = (k * s).astype(jnp.bfloat16)
        w = (k * h).astype(jnp.bfloat16)
        kernel_terms = s * h
        if has_previous:
            kernel_terms = kernel_terms + previous_ref[channel]
        if is_last:
            spread(kernel_refs, channel, kernel_terms.astype(jnp.bfloat16))
        else:
            kernel_refs[0][channel] = kernel_terms
        c = matmul(two_t, z).astype(jnp.bfloat16)
        v = matmul(two_t, w).astype(jnp.bfloat16)
        spread(grad_refs, channel, matmul(v, one).astype(jnp.bfloat16))
        first = matmul_rows(c, y) + matmul_rows(v, x)
        second = matmul_columns(z, g) + matmul_columns(w, a)
        first_sum = first if first_sum is None else first_sum + first
        second_sum = second if second_sum is None else second_sum + second
    first_ref[...] += first_sum
    second_ref[...] += second_sum


def mix(x, y, k, previous, is_last, factors):
    parts = len(k)
    channels, part_rows, width = k[0].shape
    rows = parts * part_rows
    step = math.gcd(channels, 4)
    block = pl.BlockSpec((step, part_rows, width), lambda i: (i, 0, 0))
    tall = pl.BlockSpec((step, rows, width), lambda i: (i, 0, 0))
    has_previous = previous is not None
    small = [pl.BlockSpec(f.shape, lambda i: (0, 0)) for f in factors]
    sums = [jax.ShapeDtypeStruct((width, width), jnp.float32), jax.ShapeDtypeStruct((rows, rows), jnp.float32)]
    piece = jax.ShapeDtypeStruct((channels, part_rows, width), jnp.bfloat16)
    partial = jax.ShapeDtypeStruct((channels, rows, width), jnp.float32)
    out = pl.pallas_call(
        functools.partial(mix_kernel, parts, has_previous, is_last),
        grid=(channels // step,),
        in_specs=[block] * (3 * parts) + [tall] * has_previous + small,
        out_specs=[block] * parts
        + ([block] * parts if is_last else [tall])
        + [pl.BlockSpec(s.shape, lambda i: (0, 0)) for s in sums],
        out_shape=[piece] * parts + ([piece] * parts if is_last else [partial]) + sums,
        compiler_params=pltpu.CompilerParams(
            dimension_semantics=("arbitrary",), vmem_limit_bytes=VMEM_BYTES
        ),
        cost_estimate=pl.CostEstimate(
            flops=22 * channels * rows * width * width,
            bytes_accessed=12 * channels * rows * width,
            transcendentals=0,
        ),
    )(*x, *y, *k, *((previous,) if has_previous else ()), *factors)
    return out[:parts], out[parts:-2], out[-2], out[-1]


class Sends:
    def __init__(self, parts):
        self.parts = parts
        self.results = []

    def order(self):
        half = self.parts // 2
        far, near = list(range(half, self.parts)), list(range(1, half))
        mixed = []
        while far or near:
            mixed += [q.pop(0) for q in (far, near) if q]
        return mixed

    def __call__(self, pieces, hooks=(), first_window=WINDOW):
        places = {}
        hooked = []
        for step, k in enumerate(self.order()):
            values = pieces[k]
            for at, make in hooks:
                if at == step:
                    values, made = lax.optimization_barrier((values, make()))
                    hooked.append(made)
            window = min(WINDOW, first_window + step)
            if len(self.results) >= window:
                values, self.results[-window] = lax.optimization_barrier((values, self.results[-window]))
            pairs = [(i, i ^ k) for i in range(self.parts)]
            places[k] = len(self.results)
            self.results.append(lax.ppermute(values, "seq", pairs))
        return ((pieces[0], places), *hooked) if hooks else (pieces[0], places)

    def get(self, sent):
        own, places = sent
        return [own] + [self.results[places[k]] for k in range(1, self.parts)]


def on_device(inputs, cotangent, kernel, factor_one, factor_two):
    batch_count, row_count, channels = inputs.shape
    block_size = factor_one.shape[0]
    block_count = factor_two.shape[0]
    local_blocks = row_count // block_size
    parts = lax.axis_size("seq")
    own = channels // parts
    group = min(LANES, channels) // own
    me = lax.axis_index("seq")
    me_array = me.reshape(1).astype(jnp.int32)
    send = Sends(parts)

    def pack(values, place):
        cube = values.reshape(-1, local_blocks, block_size, channels)
        pieces = []
        for lane_block in range(parts // group):
            pieces += leave(cube, place, me_array, lane_block, group)
        return pieces

    def unpack(pieces, place, count, onto):
        for lane_block in range(parts // group):
            some = pieces[lane_block * group : (lane_block + 1) * group]
            onto = arrive(some, me_array, lane_block, place, count, channels, onto)
        return onto

    def relative(values, axis):
        starts = [(me ^ k) * local_blocks for k in range(parts)]
        return jnp.concatenate([lax.dynamic_slice_in_dim(values, s, local_blocks, axis) for s in starts], axis)

    two = relative(relative(factor_two, 0), 1)
    factors = (factor_one, factor_one.T, two, two.T)
    kernel_sent = send(pack(kernel, 0))
    batch_sent = [(send(pack(inputs, n)), send(pack(cotangent, n))) for n in range(batch_count)]
    k_all = send.get(kernel_sent)
    grads_sent = []
    previous = None
    first_sum = second_sum = 0.0
    for n, (x_sent, y_sent) in enumerate(batch_sent):
        is_last = n == batch_count - 1
        grads, kernel_grads, first, second = mix(send.get(x_sent), send.get(y_sent), k_all, previous, is_last, factors)
        previous = kernel_grads[0]
        first_sum, second_sum = first_sum + first, second_sum + second
        if not is_last:
            grads_sent.append(send(grads))

    axes = ("dp", "seq")
    devices = lax.axis_size(axes)

    def reduced():
        both = jnp.concatenate([first_sum, relative(relative(second_sum, 0), 1)])
        shares = both.reshape(devices, -1, both.shape[1])
        return jnp.sum(lax.all_to_all(shares, axes, 0, 0, tiled=True), axis=0)

    def early_grads():
        done = None
        for n, sent in enumerate(grads_sent):
            done = unpack(send.get(sent), n, batch_count, done)
        return done

    kernel_sent = send(kernel_grads, first_window=2)
    steps = parts - 1
    last_sent, share, grad_inputs, grad_kernel = send(
        grads,
        (
            (0, reduced),
            (steps // 2, early_grads),
            (steps - 1, lambda: unpack(send.get(kernel_sent), 0, 1, None)),
        ),
    )
    last = send.get(last_sent)
    share, last[-1] = lax.optimization_barrier((share, last[-1]))
    copies = jnp.broadcast_to(share, (devices, *share.shape))
    totals = lax.all_to_all(copies, axes, 0, 0, tiled=True).reshape(-1, block_size)
    first_total, second_total = totals[:block_size], totals[block_size:]
    grad_inputs = unpack(last, batch_count - 1, batch_count, grad_inputs)
    full_width = channels * lax.axis_size("dp")
    scale_first = 1.0 / math.sqrt(batch_count * block_count * full_width)
    scale_second = 1.0 / math.sqrt(batch_count * block_size * full_width)
    return (
        grad_inputs.reshape(inputs.shape),
        grad_kernel.reshape(kernel.shape),
        first_total * scale_first,
        second_total * scale_second,
    )


def solution(mesh):
    return jax.shard_map(
        on_device,
        mesh=mesh,
        in_specs=(P(None, "seq", "dp"), P(None, "seq", "dp"), P("seq", "dp"), P(), P()),
        out_specs=(P(None, "seq", "dp"), P("seq", "dp"), P(), P()),
        check_vma=False,
    )
```

time: 2170 us -> 1480 us (0.68)
  waiting for transfers between devices: 1590 us -> 824 us
  starting transfers between devices: 34.5 us -> 431 us
  local copies, waits for them, and re-layouts: 255 us -> 4.45 us
  matrix products: 243 us -> 0 us
  Pallas kernels: 0 us -> 219 us
    all_to_all x6 -> x2, waiting for transfers between devices: 1480 us -> 83 us  [the longest x1 51.3 us: reduced(): return jnp.sum(lax.all_to_all(shares, axes, 0, 0, tiled=True), axis=0)]
    ppermute x0 -> x56, waiting for transfers between devices: none -> 741 us  [__call__(): self.results.append(lax.ppermute(values, 'seq', pairs))]
    ppermute x0 -> x56, starting transfers between devices: none -> 394 us  [__call__(): self.results.append(lax.ppermute(values, 'seq', pairs))]
    dot_general x11 -> x0, matrix products: 243 us -> none  [the longest x2 90.3 us: across_blocks(): jnp.einsum('ea,nach->nech', factor, values, preferred_element_type=jnp.fl...]
    pallas_call x0 -> x34, Pallas kernels: none -> 219 us  [the longest x2 110 us: mix(): pl.pallas_call(functools.partial(mix_kernel, parts, has_previous, is_last...]
    convert_element_type x7 -> x0, local copies, waits for them, and re-layouts: 159 us -> none  [the longest x2 31.5 us: on_device(): kernel_spread = lax.all_to_all(kernel_cube, 'seq', split_axis=1, concat_a...]
    psum x1 -> x0, waiting for transfers between devices: 114 us -> none  [on_device(): lax.psum((first_terms, second_terms), ('dp', 'seq'))]
    all_to_all x6 -> x0, local copies, waits for them, and re-layouts: 85.2 us -> none  [the longest x1 18.5 us: on_device(): lax.all_to_all(within_mix, 'seq', split_axis=2, concat_axis=1, tiled=True)]
  transfers between devices with their start and end apart: 7 -> 58, of which waited for: 7 -> 26; matrix products, arithmetic and copies ran while one was open for 16% -> 0% of each run, Pallas kernels for 0% -> 15%
where the time goes in v1:
time: 1480 us
  waiting for transfers between devices  824 us (56%)
  starting transfers between devices  431 us (29%)
  Pallas kernels  219 us (15%)
    ppermute x56, waiting for transfers between devices, __call__(): self.results.append(lax.ppermute(values, 'seq', pairs))  741 us
    ppermute x56, starting transfers between devices, __call__(): self.results.append(lax.ppermute(values, 'seq', pairs))  394 us
    pallas_call x2, Pallas kernels, mix(): pl.pallas_call(functools.partial(mix_kernel, parts, has_previous, is_last...  110 us
    pallas_call x20, Pallas kernels, leave(): pl.pallas_call(functools.partial(leave_kernel, group), grid_spec=pltpu.Pr...  70.2 us
    all_to_all x1, waiting for transfers between devices, reduced(): return jnp.sum(lax.all_to_all(shares, axes, 0, 0, tiled=True), axis=0)  51.3 us
    pallas_call x12, Pallas kernels, arrive(): pl.pallas_call(functools.partial(arrive_kernel, group), grid_spec=pltpu.P...  39.4 us
    all_to_all x1, waiting for transfers between devices, on_device(): lax.all_to_all(copies, axes, 0, 0, tiled=True).reshape(-1, block_size)  31.7 us
  transfers between devices with their start and end apart: 58, of which 26 were waited for; matrix products, arithmetic and copies ran while one was open for 0% of the time, Pallas kernels for 15%

profile of v1, /device:TPU:3, one launch (start us, length us, event | category | flops | bytes accessed | tf_op | source)
XLA Modules:
  0.0 1483.5 jit_solution(16352680901075582268)
XLA Ops:
  50.0 55.6 %collective-permute-done.9.refs_21_ = bf16[64,32,256]{2,1,0:T(8,128)(2,1)S(1)} collective-permute-done((bf16[64,32,256]{2,1,0:T(8,128)(2,1)}, bf16[64,32,256]{2,1,0:T(8,128)(2,1)S(1)}, u32[]{:S(2)}, u32[]{:S(2)}) %collective-permute-start.9) | collective-permute-done | bytes 1048608 | tf_op jit(solution)/shard_map/ppermute | solution.py:213
  105.6 67.5 %collective-permute-done.4.refs_20_ = bf16[64,32,256]{2,1,0:T(8,128)(2,1)} collective-permute-done((bf16[64,32,256]{2,1,0:T(8,128)(2,1)}, bf16[64,32,256]{2,1,0:T(8,128)(2,1)}, u32[]{:S(2)}, u32[]{:S(2)}) %collective-permute-start.4) | collective-permute-done | bytes 1048608 | tf_op jit(solution)/shard_map/ppermute | solution.py:213
  190.6 43.1 %collective-permute-start.1 = (bf16[64,32,256]{2,1,0:T(8,128)(2,1)}, bf16[64,32,256]{2,1,0:T(8,128)(2,1)S(1)}, u32[]{:S(2)}, u32[]{:S(2)}) collective-permute-start(bf16[64,32,256]{2,1,0:T(8,128)(2,1)} %get-tuple-element.187), channel_id=1, source_target_pairs={{0,2},{1,3},{2,0},{3,1},{4,6},{5,7},{6,4},{7,5},{8,10},{9,11},{10,... | collective-permute-start | bytes 3145736 | tf_op jit(solution)/shard_map/ppermute | solution.py:213
  242.8 42.7 %collective-permute-done.15.refs_5_ = bf16[64,32,256]{2,1,0:T(8,128)(2,1)} collective-permute-done((bf16[64,32,256]{2,1,0:T(8,128)(2,1)}, bf16[64,32,256]{2,1,0:T(8,128)(2,1)}, u32[]{:S(2)}, u32[]{:S(2)}) %collective-permute-start.15) | collective-permute-done | bytes 1048608 | tf_op jit(solution)/shard_map/ppermute | solution.py:213
  288.9 42.9 %collective-permute-start.11 = (bf16[64,32,256]{2,1,0:T(8,128)(2,1)}, bf16[64,32,256]{2,1,0:T(8,128)(2,1)}, u32[]{:S(2)}, u32[]{:S(2)}) collective-permute-start(bf16[64,32,256]{2,1,0:T(8,128)(2,1)} %get-tuple-element.209), channel_id=1, source_target_pairs={{0,4},{1,5},{2,6},{3,7},{4,0},{5,1},{6,2},{7,3},{8,12},{9,13},{10,... | collective-permute-start | bytes 3145736 | tf_op jit(solution)/shard_map/ppermute | solution.py:213
  339.0 37.8 %collective-permute-start.2 = (bf16[64,32,256]{2,1,0:T(8,128)(2,1)}, bf16[64,32,256]{2,1,0:T(8,128)(2,1)}, u32[]{:S(2)}, u32[]{:S(2)}) collective-permute-start(bf16[64,32,256]{2,1,0:T(8,128)(2,1)} %get-tuple-element.188), channel_id=1, source_target_pairs={{0,5},{1,4},{2,7},{3,6},{4,1},{5,0},{6,3},{7,2},{8,13},{9,12},{10,... | collective-permute-start | bytes 3145736 | tf_op jit(solution)/shard_map/ppermute | solution.py:213
  376.8 47.0 %collective-permute-start.20 = (bf16[64,32,256]{2,1,0:T(8,128)(2,1)}, bf16[64,32,256]{2,1,0:T(8,128)(2,1)}, u32[]{:S(2)}, u32[]{:S(2)}) collective-permute-start(bf16[64,32,256]{2,1,0:T(8,128)(2,1)} %get-tuple-element.228), channel_id=1, source_target_pairs={{0,2},{1,3},{2,0},{3,1},{4,6},{5,7},{6,4},{7,5},{8,10},{9,11},{10,... | collective-permute-start | bytes 3145736 | tf_op jit(solution)/shard_map/ppermute | solution.py:213
  470.3 26.1 %collective-permute-done.20.refs_10_ = bf16[64,32,256]{2,1,0:T(8,128)(2,1)} collective-permute-done((bf16[64,32,256]{2,1,0:T(8,128)(2,1)}, bf16[64,32,256]{2,1,0:T(8,128)(2,1)}, u32[]{:S(2)}, u32[]{:S(2)}) %collective-permute-start.20) | collective-permute-done | bytes 1048608 | tf_op jit(solution)/shard_map/ppermute | solution.py:213
  496.4 84.5 %collective-permute-done.25.refs_11_ = bf16[64,32,256]{2,1,0:T(8,128)(2,1)} collective-permute-done((bf16[64,32,256]{2,1,0:T(8,128)(2,1)}, bf16[64,32,256]{2,1,0:T(8,128)(2,1)}, u32[]{:S(2)}, u32[]{:S(2)}) %collective-permute-start.25) | collective-permute-done | bytes 1048608 | tf_op jit(solution)/shard_map/ppermute | solution.py:213
  595.6 75.6 %collective-permute-start.13 = (bf16[64,32,256]{2,1,0:T(8,128)(2,1)}, bf16[64,32,256]{2,1,0:T(8,128)(2,1)}, u32[]{:S(2)}, u32[]{:S(2)}) collective-permute-start(bf16[64,32,256]{2,1,0:T(8,128)(2,1)} %get-tuple-element.211), channel_id=1, source_target_pairs={{0,3},{1,2},{2,1},{3,0},{4,7},{5,6},{6,5},{7,4},{8,11},{9,10},{10,... | collective-permute-start | bytes 3145736 | tf_op jit(solution)/shard_map/ppermute | solution.py:213
  703.7 57.6 %collective-permute-start.29 = (bf16[64,32,256]{2,1,0:T(8,128)(2,1)}, bf16[64,32,256]{2,1,0:T(8,128)(2,1)}, u32[]{:S(2)}, u32[]{:S(2)}) collective-permute-start(bf16[64,32,256]{2,1,0:T(8,128)(2,1)} %get-tuple-element.274), channel_id=1, source_target_pairs={{0,2},{1,3},{2,0},{3,1},{4,6},{5,7},{6,4},{7,5},{8,10},{9,11},{10,... | collective-permute-start | bytes 3145736 | tf_op jit(solution)/shard_map/ppermute | solution.py:213
  784.6 54.3 %shard_map.104 = (bf16[64,32,256]{2,1,0:T(8,128)(2,1)}, bf16[64,32,256]{2,1,0:T(8,128)(2,1)}, bf16[64,32,256]{2,1,0:T(8,128)(2,1)}, bf16[64,32,256]{2,1,0:T(8,12...) custom-call(bf16[64,32,256]{2,1,0:T(8,128)(2,1)} %get-tuple-element., ...), custom_call_target="tpu_custom_call" | custom-call | flops 23622320128 | bytes 50331648 | tf_op jit(solution)/shard_map/pallas_call | solution.py:166
  854.9 63.3 %collective-permute-done.32.refs_13_ = bf16[64,32,256]{2,1,0:T(8,128)(2,1)} collective-permute-done((bf16[64,32,256]{2,1,0:T(8,128)(2,1)S(1)}, bf16[64,32,256]{2,1,0:T(8,128)(2,1)}, u32[]{:S(2)}, u32[]{:S(2)}) %collective-permute-start.32) | collective-permute-done | bytes 1048608 | tf_op jit(solution)/shard_map/ppermute | solution.py:213
  918.3 22.7 %collective-permute-start.42 = (bf16[64,32,256]{2,1,0:T(8,128)(2,1)}, bf16[64,32,256]{2,1,0:T(8,128)(2,1)S(1)}, u32[]{:S(2)}, u32[]{:S(2)}) collective-permute-start(bf16[64,32,256]{2,1,0:T(8,128)(2,1)} %get-tuple-element.317), channel_id=1, source_target_pairs={{0,3},{1,2},{2,1},{3,0},{4,7},{5,6},{6,5},{7,4},{8,11},{9,10},{10,... | collective-permute-start | bytes 3145736 | tf_op jit(solution)/shard_map/ppermute | solution.py:213
  964.2 55.3 %shard_map.105 = (bf16[64,32,256]{2,1,0:T(8,128)(2,1)}, bf16[64,32,256]{2,1,0:T(8,128)(2,1)}, bf16[64,32,256]{2,1,0:T(8,128)(2,1)}, bf16[64,32,256]{2,1,0:T(8,12...) custom-call(bf16[64,32,256]{2,1,0:T(8,128)(2,1)} %get-tuple-element., ...), custom_call_target="tpu_custom_call" | custom-call | flops 23622320128 | bytes 50331648 | tf_op jit(solution)/shard_map/pallas_call | solution.py:166
  1022.4 30.7 %collective-permute-done.41.refs_0_ = bf16[64,32,256]{2,1,0:T(8,128)(2,1)} collective-permute-done((bf16[64,32,256]{2,1,0:T(8,128)(2,1)}, bf16[64,32,256]{2,1,0:T(8,128)(2,1)}, u32[]{:S(2)}, u32[]{:S(2)}) %collective-permute-start.41) | collective-permute-done | bytes 1048608 | tf_op jit(solution)/shard_map/ppermute | solution.py:213
  1053.3 22.5 %collective-permute-start.45 = (bf16[64,32,256]{2,1,0:T(8,128)(2,1)}, bf16[64,32,256]{2,1,0:T(8,128)(2,1)}, u32[]{:S(2)}, u32[]{:S(2)}) collective-permute-start(bf16[64,32,256]{2,1,0:T(8,128)(2,1)} %get-tuple-element.330), channel_id=1, source_target_pairs={{0,4},{1,5},{2,6},{3,7},{4,0},{5,1},{6,2},{7,3},{8,12},{9,13},{10,... | collective-permute-start | bytes 3145736 | tf_op jit(solution)/shard_map/ppermute | solution.py:213
  1087.6 61.0 %collective-permute-done.40.refs_1_ = bf16[64,32,256]{2,1,0:T(8,128)(2,1)S(1)} collective-permute-done((bf16[64,32,256]{2,1,0:T(8,128)(2,1)}, bf16[64,32,256]{2,1,0:T(8,128)(2,1)S(1)}, u32[]{:S(2)}, u32[]{:S(2)}) %collective-permute-start.40) | collective-permute-done | bytes 1048608 | tf_op jit(solution)/shard_map/ppermute | solution.py:213
  1174.5 51.3 %all-to-all-done = f32[32,16,256]{2,1,0:T(8,128)S(1)} async-done(((f32[32,16,256]{2,1,0:T(8,128)}), f32[32,16,256]{2,1,0:T(8,128)S(1)}, u32[]{:S(2)}, u32[]{:S(2)}) %all-to-all-start) | async-done | bytes 524320 | tf_op jit(solution)/shard_map/all_to_all | solution.py:272
  1239.0 27.7 %collective-permute-done.47.refs_1_ = bf16[64,32,256]{2,1,0:T(8,128)(2,1)} collective-permute-done((bf16[64,32,256]{2,1,0:T(8,128)(2,1)}, bf16[64,32,256]{2,1,0:T(8,128)(2,1)}, u32[]{:S(2)}, u32[]{:S(2)}) %collective-permute-start.47) | collective-permute-done | bytes 1048608 | tf_op jit(solution)/shard_map/ppermute | solution.py:213
  1279.9 53.2 %collective-permute-done.50.refs_0_ = bf16[64,32,256]{2,1,0:T(8,128)(2,1)S(1)} collective-permute-done((bf16[64,32,256]{2,1,0:T(8,128)(2,1)}, bf16[64,32,256]{2,1,0:T(8,128)(2,1)S(1)}, u32[]{:S(2)}, u32[]{:S(2)}) %collective-permute-start.50) | collective-permute-done | bytes 1048608 | tf_op jit(solution)/shard_map/ppermute | solution.py:213
  1360.4 27.9 %all-to-all-start.1 = ((f32[32,16,256]{2,1,0:T(8,128)}), f32[32,16,256]{2,1,0:T(8,128)S(1)}, u32[]{:S(2)}, u32[]{:S(2)}) async-start(f32[32,16,256]{2,1,0:T(8,128)} %broadcast_in_dim.3), calls=%async_computation.1 | async-start | bytes 1048576 | tf_op jit(solution)/shard_map/all_to_all | solution.py:293
  1407.1 23.7 %collective-permute-done.54.refs_1_ = bf16[64,32,256]{2,1,0:T(8,128)(2,1)} collective-permute-done((bf16[64,32,256]{2,1,0:T(8,128)(2,1)}, bf16[64,32,256]{2,1,0:T(8,128)(2,1)}, u32[]{:S(2)}, u32[]{:S(2)}) %collective-permute-start.54) | collective-permute-done | bytes 1048608 | tf_op jit(solution)/shard_map/ppermute | solution.py:213
  1450.9 31.7 %all-to-all-done.1 = f32[32,16,256]{2,1,0:T(8,128)S(1)} async-done(((f32[32,16,256]{2,1,0:T(8,128)}), f32[32,16,256]{2,1,0:T(8,128)S(1)}, u32[]{:S(2)}, u32[]{:S(2)}) %all-to-all-start.1) | async-done | bytes 524320 | tf_op jit(solution)/shard_map/all_to_all | solution.py:293
  (204 shorter events, 376.7 us)
Async XLA Ops:
  16.0 157.2 %collective-permute-start.4 = (bf16[64,32,256]{2,1,0:T(8,128)(2,1)}, bf16[64,32,256]{2,1,0:T(8,128)(2,1)}, u32[]{:S(2)}, u32[]{:S(2)}) collective-permute-start(bf16[64,32,256]{2,1,0:T(8,128)(2,1)} %get-tuple-element.196), channel_id=1, source_target_pairs={{0,4},{1,5},{2,6},{3,7},{4,0},{5,1},{6,2},{7,3},{8,12},{9,13},{10,... | collective-permute-start | bytes 3145736 | tf_op jit(solution)/shard_map/ppermute | solution.py:213
  19.5 153.9 %collective-permute-start = (bf16[64,32,256]{2,1,0:T(8,128)(2,1)}, bf16[64,32,256]{2,1,0:T(8,128)(2,1)}, u32[]{:S(2)}, u32[]{:S(2)}) collective-permute-start(bf16[64,32,256]{2,1,0:T(8,128)(2,1)} %get-tuple-element.186), channel_id=1, source_target_pairs={{0,6},{1,7},{2,4},{3,5},{4,2},{5,3},{6,0},{7,1},{8,14},{9,15},{10,... | collective-permute-start | bytes 3145736 | tf_op jit(solution)/shard_map/ppermute | solution.py:213
  47.2 143.5 %collective-permute-start.18 = (bf16[64,32,256]{2,1,0:T(8,128)(2,1)}, bf16[64,32,256]{2,1,0:T(8,128)(2,1)}, u32[]{:S(2)}, u32[]{:S(2)}) collective-permute-start(bf16[64,32,256]{2,1,0:T(8,128)(2,1)} %get-tuple-element.226), channel_id=1, source_target_pairs={{0,3},{1,2},{2,1},{3,0},{4,7},{5,6},{6,5},{7,4},{8,11},{9,10},{10,... | collective-permute-start | bytes 3145736 | tf_op jit(solution)/shard_map/ppermute | solution.py:213
  49.8 190.8 %collective-permute-start.23 = (bf16[64,32,256]{2,1,0:T(8,128)(2,1)}, bf16[64,32,256]{2,1,0:T(8,128)(2,1)}, u32[]{:S(2)}, u32[]{:S(2)}) collective-permute-start(bf16[64,32,256]{2,1,0:T(8,128)(2,1)} %get-tuple-element.237), channel_id=1, source_target_pairs={{0,4},{1,5},{2,6},{3,7},{4,0},{5,1},{6,2},{7,3},{8,12},{9,13},{10,... | collective-permute-start | bytes 3145736 | tf_op jit(solution)/shard_map/ppermute | solution.py:213
  105.6 179.9 %collective-permute-start.15 = (bf16[64,32,256]{2,1,0:T(8,128)(2,1)}, bf16[64,32,256]{2,1,0:T(8,128)(2,1)}, u32[]{:S(2)}, u32[]{:S(2)}) collective-permute-start(bf16[64,32,256]{2,1,0:T(8,128)(2,1)} %get-tuple-element.218), channel_id=1, source_target_pairs={{0,5},{1,4},{2,7},{3,6},{4,1},{5,0},{6,3},{7,2},{8,13},{9,12},{10,... | collective-permute-start | bytes 3145736 | tf_op jit(solution)/shard_map/ppermute | solution.py:213
  190.6 148.3 %collective-permute-start.1 = (bf16[64,32,256]{2,1,0:T(8,128)(2,1)}, bf16[64,32,256]{2,1,0:T(8,128)(2,1)S(1)}, u32[]{:S(2)}, u32[]{:S(2)}) collective-permute-start(bf16[64,32,256]{2,1,0:T(8,128)(2,1)} %get-tuple-element.187), channel_id=1, source_target_pairs={{0,2},{1,3},{2,0},{3,1},{4,6},{5,7},{6,4},{7,5},{8,10},{9,11},{10,... | collective-permute-start | bytes 3145736 | tf_op jit(solution)/shard_map/ppermute | solution.py:213
  288.7 135.2 %collective-permute-start.16 = (bf16[64,32,256]{2,1,0:T(8,128)(2,1)}, bf16[64,32,256]{2,1,0:T(8,128)(2,1)}, u32[]{:S(2)}, u32[]{:S(2)}) collective-permute-start(bf16[64,32,256]{2,1,0:T(8,128)(2,1)} %get-tuple-element.219), channel_id=1, source_target_pairs={{0,1},{1,0},{2,3},{3,2},{4,5},{5,4},{6,7},{7,6},{8,9},{9,8},{10,11... | collective-permute-start | bytes 3145736 | tf_op jit(solution)/shard_map/ppermute | solution.py:213
  288.9 156.3 %collective-permute-start.11 = (bf16[64,32,256]{2,1,0:T(8,128)(2,1)}, bf16[64,32,256]{2,1,0:T(8,128)(2,1)}, u32[]{:S(2)}, u32[]{:S(2)}) collective-permute-start(bf16[64,32,256]{2,1,0:T(8,128)(2,1)} %get-tuple-element.209), channel_id=1, source_target_pairs={{0,4},{1,5},{2,6},{3,7},{4,0},{5,1},{6,2},{7,3},{8,12},{9,13},{10,... | collective-permute-start | bytes 3145736 | tf_op jit(solution)/shard_map/ppermute | solution.py:213
  339.0 131.3 %collective-permute-start.2 = (bf16[64,32,256]{2,1,0:T(8,128)(2,1)}, bf16[64,32,256]{2,1,0:T(8,128)(2,1)}, u32[]{:S(2)}, u32[]{:S(2)}) collective-permute-start(bf16[64,32,256]{2,1,0:T(8,128)(2,1)} %get-tuple-element.188), channel_id=1, source_target_pairs={{0,5},{1,4},{2,7},{3,6},{4,1},{5,0},{6,3},{7,2},{8,13},{9,12},{10,... | collective-permute-start | bytes 3145736 | tf_op jit(solution)/shard_map/ppermute | solution.py:213
  423.8 157.0 %collective-permute-start.25 = (bf16[64,32,256]{2,1,0:T(8,128)(2,1)}, bf16[64,32,256]{2,1,0:T(8,128)(2,1)}, u32[]{:S(2)}, u32[]{:S(2)}) collective-permute-start(bf16[64,32,256]{2,1,0:T(8,128)(2,1)} %get-tuple-element.239), channel_id=1, source_target_pairs={{0,3},{1,2},{2,1},{3,0},{4,7},{5,6},{6,5},{7,4},{8,11},{9,10},{10,... | collective-permute-start | bytes 3145736 | tf_op jit(solution)/shard_map/ppermute | solution.py:213
  445.3 135.6 %collective-permute-start.17 = (bf16[64,32,256]{2,1,0:T(8,128)(2,1)}, bf16[64,32,256]{2,1,0:T(8,128)(2,1)S(1)}, u32[]{:S(2)}, u32[]{:S(2)}) collective-permute-start(bf16[64,32,256]{2,1,0:T(8,128)(2,1)} %get-tuple-element.220), channel_id=1, source_target_pairs={{0,4},{1,5},{2,6},{3,7},{4,0},{5,1},{6,2},{7,3},{8,12},{9,13},{10,... | collective-permute-start | bytes 3145736 | tf_op jit(solution)/shard_map/ppermute | solution.py:213
  455.7 137.0 %collective-permute-start.12 = (bf16[64,32,256]{2,1,0:T(8,128)(2,1)}, bf16[64,32,256]{2,1,0:T(8,128)(2,1)}, u32[]{:S(2)}, u32[]{:S(2)}) collective-permute-start(bf16[64,32,256]{2,1,0:T(8,128)(2,1)} %get-tuple-element.210), channel_id=1, source_target_pairs={{0,7},{1,6},{2,5},{3,4},{4,3},{5,2},{6,1},{7,0},{8,15},{9,14},{10,... | collective-permute-start | bytes 3145736 | tf_op jit(solution)/shard_map/ppermute | solution.py:213
  470.3 125.4 %collective-permute-start.7 = (bf16[64,32,256]{2,1,0:T(8,128)(2,1)}, bf16[64,32,256]{2,1,0:T(8,128)(2,1)}, u32[]{:S(2)}, u32[]{:S(2)}) collective-permute-start(bf16[64,32,256]{2,1,0:T(8,128)(2,1)} %get-tuple-element.199), channel_id=1, source_target_pairs={{0,6},{1,7},{2,4},{3,5},{4,2},{5,3},{6,0},{7,1},{8,14},{9,15},{10,... | collective-permute-start | bytes 3145736 | tf_op jit(solution)/shard_map/ppermute | solution.py:213
  496.4 174.9 %collective-permute-start.3 = (bf16[64,32,256]{2,1,0:T(8,128)(2,1)}, bf16[64,32,256]{2,1,0:T(8,128)(2,1)S(1)}, u32[]{:S(2)}, u32[]{:S(2)}) collective-permute-start(bf16[64,32,256]{2,1,0:T(8,128)(2,1)} %get-tuple-element.189), channel_id=1, source_target_pairs={{0,1},{1,0},{2,3},{3,2},{4,5},{5,4},{6,7},{7,6},{8,9},{9,8},{10,11... | collective-permute-start | bytes 3145736 | tf_op jit(solution)/shard_map/ppermute | solution.py:213
  595.6 165.6 %collective-permute-start.13 = (bf16[64,32,256]{2,1,0:T(8,128)(2,1)}, bf16[64,32,256]{2,1,0:T(8,128)(2,1)}, u32[]{:S(2)}, u32[]{:S(2)}) collective-permute-start(bf16[64,32,256]{2,1,0:T(8,128)(2,1)} %get-tuple-element.211), channel_id=1, source_target_pairs={{0,3},{1,2},{2,1},{3,0},{4,7},{5,6},{6,5},{7,4},{8,11},{9,10},{10,... | collective-permute-start | bytes 3145736 | tf_op jit(solution)/shard_map/ppermute | solution.py:213
  703.7 135.2 %collective-permute-start.29 = (bf16[64,32,256]{2,1,0:T(8,128)(2,1)}, bf16[64,32,256]{2,1,0:T(8,128)(2,1)}, u32[]{:S(2)}, u32[]{:S(2)}) collective-permute-start(bf16[64,32,256]{2,1,0:T(8,128)(2,1)} %get-tuple-element.274), channel_id=1, source_target_pairs={{0,2},{1,3},{2,0},{3,1},{4,6},{5,7},{6,4},{7,5},{8,10},{9,11},{10,... | collective-permute-start | bytes 3145736 | tf_op jit(solution)/shard_map/ppermute | solution.py:213
  761.2 157.0 %collective-permute-start.33 = (bf16[64,32,256]{2,1,0:T(8,128)(2,1)}, bf16[64,32,256]{2,1,0:T(8,128)(2,1)}, u32[]{:S(2)}, u32[]{:S(2)}) collective-permute-start(bf16[64,32,256]{2,1,0:T(8,128)(2,1)} %get-tuple-element.286), channel_id=1, source_target_pairs={{0,6},{1,7},{2,4},{3,5},{4,2},{5,3},{6,0},{7,1},{8,14},{9,15},{10,... | collective-permute-start | bytes 3145736 | tf_op jit(solution)/shard_map/ppermute | solution.py:213
  782.5 135.8 %collective-permute-start.32 = (bf16[64,32,256]{2,1,0:T(8,128)(2,1)S(1)}, bf16[64,32,256]{2,1,0:T(8,128)(2,1)}, u32[]{:S(2)}, u32[]{:S(2)}) collective-permute-start(bf16[64,32,256]{2,1,0:T(8,128)(2,1)S(1)} %copy-done.19), channel_id=1, source_target_pairs={{0,5},{1,4},{2,7},{3,6},{4,1},{5,0},{6,3},{7,2},{8,13},{9,12},{10,... | collective-permute-start | bytes 3145736 | tf_op jit(solution)/shard_map/ppermute | solution.py:213
  782.7 135.6 %collective-permute-start.34 = (bf16[64,32,256]{2,1,0:T(8,128)(2,1)}, bf16[64,32,256]{2,1,0:T(8,128)(2,1)}, u32[]{:S(2)}, u32[]{:S(2)}) collective-permute-start(bf16[64,32,256]{2,1,0:T(8,128)(2,1)} %get-tuple-element.289), channel_id=1, source_target_pairs={{0,7},{1,6},{2,5},{3,4},{4,3},{5,2},{6,1},{7,0},{8,15},{9,14},{10,... | collective-permute-start | bytes 3145736 | tf_op jit(solution)/shard_map/ppermute | solution.py:213
  942.2 143.2 %collective-permute-start.39 = (bf16[64,32,256]{2,1,0:T(8,128)(2,1)}, bf16[64,32,256]{2,1,0:T(8,128)(2,1)}, u32[]{:S(2)}, u32[]{:S(2)}) collective-permute-start(bf16[64,32,256]{2,1,0:T(8,128)(2,1)} %get-tuple-element.307), channel_id=1, source_target_pairs={{0,6},{1,7},{2,4},{3,5},{4,2},{5,3},{6,0},{7,1},{8,14},{9,15},{10,... | collective-permute-start | bytes 3145736 | tf_op jit(solution)/shard_map/ppermute | solution.py:213
  1022.4 126.2 %collective-permute-start.40 = (bf16[64,32,256]{2,1,0:T(8,128)(2,1)}, bf16[64,32,256]{2,1,0:T(8,128)(2,1)S(1)}, u32[]{:S(2)}, u32[]{:S(2)}) collective-permute-start(bf16[64,32,256]{2,1,0:T(8,128)(2,1)} %get-tuple-element.310), channel_id=1, source_target_pairs={{0,5},{1,4},{2,7},{3,6},{4,1},{5,0},{6,3},{7,2},{8,13},{9,12},{10,... | collective-permute-start | bytes 3145736 | tf_op jit(solution)/shard_map/ppermute | solution.py:213
  1053.1 172.7 %collective-permute-start.48 = (bf16[64,32,256]{2,1,0:T(8,128)(2,1)}, bf16[64,32,256]{2,1,0:T(8,128)(2,1)}, u32[]{:S(2)}, u32[]{:S(2)}) collective-permute-start(bf16[64,32,256]{2,1,0:T(8,128)(2,1)} %get-tuple-element.338), channel_id=1, source_target_pairs={{0,2},{1,3},{2,0},{3,1},{4,6},{5,7},{6,4},{7,5},{8,10},{9,11},{10,... | collective-permute-start | bytes 3145736 | tf_op jit(solution)/shard_map/ppermute | solution.py:213
  1076.7 149.1 %all-to-all-start = ((f32[32,16,256]{2,1,0:T(8,128)}), f32[32,16,256]{2,1,0:T(8,128)S(1)}, u32[]{:S(2)}, u32[]{:S(2)}) async-start(f32[32,16,256]{2,1,0:T(8,128)} %bitcast.6), calls=%async_computation | async-start | bytes 1048576 | tf_op jit(solution)/shard_map/all_to_all | solution.py:272
  1085.4 181.3 %collective-permute-start.47 = (bf16[64,32,256]{2,1,0:T(8,128)(2,1)}, bf16[64,32,256]{2,1,0:T(8,128)(2,1)}, u32[]{:S(2)}, u32[]{:S(2)}) collective-permute-start(bf16[64,32,256]{2,1,0:T(8,128)(2,1)} %get-tuple-element.335), channel_id=1, source_target_pairs={{0,5},{1,4},{2,7},{3,6},{4,1},{5,0},{6,3},{7,2},{8,13},{9,12},{10,... | collective-permute-start | bytes 3145736 | tf_op jit(solution)/shard_map/ppermute | solution.py:213
  (55 other events, 4795.2 us)

commit v2 on v1

--- a/solution.py
+++ b/solution.py
@@ -108,6 +108,7 @@
     kernel_refs = take(parts if is_last else 1)
     first_ref, second_ref = refs
     channel_count, part_rows, width = x_refs[0].shape
+    rows = parts * part_rows
 
     @pl.when(pl.program_id(0) == 0)
     def _():
@@ -122,17 +123,19 @@
             ref[channel] = values[part * part_rows : (part + 1) * part_rows]
 
     one, one_t, two, two_t = one_ref[...], one_t_ref[...], two_ref[...], two_t_ref[...]
-    first_sum = None
-    second_sum = None
-    for channel in range(channel_count):
-        x, y = whole(x_refs, channel), whole(y_refs, channel)
+    channels = range(channel_count)
+    x = [whole(x_refs, channel) for channel in channels]
+    y = [whole(y_refs, channel) for channel in channels]
+    within = matmul(jnp.concatenate(x + y), one_t).astype(jnp.bfloat16)
+    a = [within[i * rows : (i + 1) * rows] for i in channels]
+    g = [within[(channel_count + i) * rows : (channel_count + i + 1) * rows] for i in channels]
+    z, w, c, v = [], [], [], []
+    for channel in channels:
         k = whole(k_refs, channel).astype(jnp.float32)
-        a = matmul(x, one_t).astype(jnp.bfloat16)
-        g = matmul(y, one_t).astype(jnp.bfloat16)
-        s = matmul(two, a).astype(jnp.bfloat16).astype(jnp.float32)
-        h = matmul(two, g).astype(jnp.bfloat16).astype(jnp.float32)
-        z = (k * s).astype(jnp.bfloat16)
-        w = (k * h).astype(jnp.bfloat16)
+        s = matmul(two, a[channel]).astype(jnp.bfloat16).astype(jnp.float32)
+        h = matmul(two, g[channel]).astype(jnp.bfloat16).astype(jnp.float32)
+        z.append((k * s).astype(jnp.bfloat16))
+        w.append((k * h).astype(jnp.bfloat16))
         kernel_terms = s * h
         if has_previous:
             kernel_terms = kernel_terms + previous_ref[channel]
@@ -140,15 +143,13 @@
             spread(kernel_refs, channel, kernel_terms.astype(jnp.bfloat16))
         else:
             kernel_refs[0][channel] = kernel_terms
-        c = matmul(two_t, z).astype(jnp.bfloat16)
-        v = matmul(two_t, w).astype(jnp.bfloat16)
-        spread(grad_refs, channel, matmul(v, one).astype(jnp.bfloat16))
-        first = matmul_rows(c, y) + matmul_rows(v, x)
-        second = matmul_columns(z, g) + matmul_columns(w, a)
-        first_sum = first if first_sum is None else first_sum + first
-        second_sum = second if second_sum is None else second_sum + second
-    first_ref[...] += first_sum
-    second_ref[...] += second_sum
+        c.append(matmul(two_t, z[channel]).astype(jnp.bfloat16))
+        v.append(matmul(two_t, w[channel]).astype(jnp.bfloat16))
+    grad = matmul(jnp.concatenate(v), one).astype(jnp.bfloat16)
+    for channel in channels:
+        spread(grad_refs, channel, grad[channel * rows : (channel + 1) * rows])
+    first_ref[...] += matmul_rows(jnp.concatenate(c + v), jnp.concatenate(y + x))
+    second_ref[...] += matmul_columns(jnp.concatenate(z + w, axis=1), jnp.concatenate(g + a, axis=1))
 
 
 def mix(x, y, k, previous, is_last, factors):

time: 1480 us -> 1480 us (level)
  Pallas kernels: 219 us -> 195 us
  waiting for transfers between devices: 824 us -> 848 us
    ppermute x56, waiting for transfers between devices: 741 us -> 765 us  [__call__(): self.results.append(lax.ppermute(values, 'seq', pairs))]
    pallas_call x2, Pallas kernels: 110 us -> 85.7 us  [mix(): pl.pallas_call(functools.partial(mix_kernel, parts, has_previous, is_last...]
  transfers between devices with their start and end apart: 58 -> 58, of which waited for: 26 -> 26; matrix products, arithmetic and copies ran while one was open for 0% -> 0% of each run, Pallas kernels for 15% -> 13%
where the time goes in v2:
time: 1480 us
  waiting for transfers between devices  848 us (57%)
  starting transfers between devices  431 us (29%)
  Pallas kernels  195 us (13%)
    ppermute x56, waiting for transfers between devices, __call__(): self.results.append(lax.ppermute(values, 'seq', pairs))  765 us
    ppermute x56, starting transfers between devices, __call__(): self.results.append(lax.ppermute(values, 'seq', pairs))  394 us
    pallas_call x2, Pallas kernels, mix(): pl.pallas_call(functools.partial(mix_kernel, parts, has_previous, is_last...  85.7 us
    pallas_call x20, Pallas kernels, leave(): pl.pallas_call(functools.partial(leave_kernel, group), grid_spec=pltpu.Pr...  70.2 us
    all_to_all x1, waiting for transfers between devices, reduced(): return jnp.sum(lax.all_to_all(shares, axes, 0, 0, tiled=True), axis=0)  51.3 us
    pallas_call x12, Pallas kernels, arrive(): pl.pallas_call(functools.partial(arrive_kernel, group), grid_spec=pltpu.P...  39.4 us
    all_to_all x1, waiting for transfers between devices, on_device(): lax.all_to_all(copies, axes, 0, 0, tiled=True).reshape(-1, block_size)  31.7 us
  transfers between devices with their start and end apart: 58, of which 26 were waited for; matrix products, arithmetic and copies ran while one was open for 0% of the time, Pallas kernels for 13%

profile of v2, /device:TPU:3, one launch (start us, length us, event | category | flops | bytes accessed | tf_op | source)
XLA Modules:
  0.0 1483.5 jit_solution(13682353943150248433)
XLA Ops:
  50.0 55.6 %collective-permute-done.9.refs_21_ = bf16[64,32,256]{2,1,0:T(8,128)(2,1)S(1)} collective-permute-done((bf16[64,32,256]{2,1,0:T(8,128)(2,1)}, bf16[64,32,256]{2,1,0:T(8,128)(2,1)S(1)}, u32[]{:S(2)}, u32[]{:S(2)}) %collective-permute-start.9) | collective-permute-done | bytes 1048608 | tf_op jit(solution)/shard_map/ppermute | solution.py:214
  105.6 67.5 %collective-permute-done.4.refs_20_ = bf16[64,32,256]{2,1,0:T(8,128)(2,1)} collective-permute-done((bf16[64,32,256]{2,1,0:T(8,128)(2,1)}, bf16[64,32,256]{2,1,0:T(8,128)(2,1)}, u32[]{:S(2)}, u32[]{:S(2)}) %collective-permute-start.4) | collective-permute-done | bytes 1048608 | tf_op jit(solution)/shard_map/ppermute | solution.py:214
  190.6 43.1 %collective-permute-start.1 = (bf16[64,32,256]{2,1,0:T(8,128)(2,1)}, bf16[64,32,256]{2,1,0:T(8,128)(2,1)S(1)}, u32[]{:S(2)}, u32[]{:S(2)}) collective-permute-start(bf16[64,32,256]{2,1,0:T(8,128)(2,1)} %get-tuple-element.187), channel_id=1, source_target_pairs={{0,2},{1,3},{2,0},{3,1},{4,6},{5,7},{6,4},{7,5},{8,10},{9,11},{10,... | collective-permute-start | bytes 3145736 | tf_op jit(solution)/shard_map/ppermute | solution.py:214
  242.8 42.7 %collective-permute-done.15.refs_5_ = bf16[64,32,256]{2,1,0:T(8,128)(2,1)} collective-permute-done((bf16[64,32,256]{2,1,0:T(8,128)(2,1)}, bf16[64,32,256]{2,1,0:T(8,128)(2,1)}, u32[]{:S(2)}, u32[]{:S(2)}) %collective-permute-start.15) | collective-permute-done | bytes 1048608 | tf_op jit(solution)/shard_map/ppermute | solution.py:214
  288.9 42.9 %collective-permute-start.11 = (bf16[64,32,256]{2,1,0:T(8,128)(2,1)}, bf16[64,32,256]{2,1,0:T(8,128)(2,1)}, u32[]{:S(2)}, u32[]{:S(2)}) collective-permute-start(bf16[64,32,256]{2,1,0:T(8,128)(2,1)} %get-tuple-element.209), channel_id=1, source_target_pairs={{0,4},{1,5},{2,6},{3,7},{4,0},{5,1},{6,2},{7,3},{8,12},{9,13},{10,... | collective-permute-start | bytes 3145736 | tf_op jit(solution)/shard_map/ppermute | solution.py:214
  339.0 37.8 %collective-permute-start.2 = (bf16[64,32,256]{2,1,0:T(8,128)(2,1)}, bf16[64,32,256]{2,1,0:T(8,128)(2,1)}, u32[]{:S(2)}, u32[]{:S(2)}) collective-permute-start(bf16[64,32,256]{2,1,0:T(8,128)(2,1)} %get-tuple-element.188), channel_id=1, source_target_pairs={{0,5},{1,4},{2,7},{3,6},{4,1},{5,0},{6,3},{7,2},{8,13},{9,12},{10,... | collective-permute-start | bytes 3145736 | tf_op jit(solution)/shard_map/ppermute | solution.py:214
  376.8 47.0 %collective-permute-start.20 = (bf16[64,32,256]{2,1,0:T(8,128)(2,1)}, bf16[64,32,256]{2,1,0:T(8,128)(2,1)}, u32[]{:S(2)}, u32[]{:S(2)}) collective-permute-start(bf16[64,32,256]{2,1,0:T(8,128)(2,1)} %get-tuple-element.228), channel_id=1, source_target_pairs={{0,2},{1,3},{2,0},{3,1},{4,6},{5,7},{6,4},{7,5},{8,10},{9,11},{10,... | collective-permute-start | bytes 3145736 | tf_op jit(solution)/shard_map/ppermute | solution.py:214
  470.3 26.1 %collective-permute-done.20.refs_10_ = bf16[64,32,256]{2,1,0:T(8,128)(2,1)} collective-permute-done((bf16[64,32,256]{2,1,0:T(8,128)(2,1)}, bf16[64,32,256]{2,1,0:T(8,128)(2,1)}, u32[]{:S(2)}, u32[]{:S(2)}) %collective-permute-start.20) | collective-permute-done | bytes 1048608 | tf_op jit(solution)/shard_map/ppermute | solution.py:214
  496.4 84.5 %collective-permute-done.25.refs_11_ = bf16[64,32,256]{2,1,0:T(8,128)(2,1)} collective-permute-done((bf16[64,32,256]{2,1,0:T(8,128)(2,1)}, bf16[64,32,256]{2,1,0:T(8,128)(2,1)}, u32[]{:S(2)}, u32[]{:S(2)}) %collective-permute-start.25) | collective-permute-done | bytes 1048608 | tf_op jit(solution)/shard_map/ppermute | solution.py:214
  595.6 75.6 %collective-permute-start.13 = (bf16[64,32,256]{2,1,0:T(8,128)(2,1)}, bf16[64,32,256]{2,1,0:T(8,128)(2,1)}, u32[]{:S(2)}, u32[]{:S(2)}) collective-permute-start(bf16[64,32,256]{2,1,0:T(8,128)(2,1)} %get-tuple-element.211), channel_id=1, source_target_pairs={{0,3},{1,2},{2,1},{3,0},{4,7},{5,6},{6,5},{7,4},{8,11},{9,10},{10,... | collective-permute-start | bytes 3145736 | tf_op jit(solution)/shard_map/ppermute | solution.py:214
  703.7 57.6 %collective-permute-start.29 = (bf16[64,32,256]{2,1,0:T(8,128)(2,1)}, bf16[64,32,256]{2,1,0:T(8,128)(2,1)}, u32[]{:S(2)}, u32[]{:S(2)}) collective-permute-start(bf16[64,32,256]{2,1,0:T(8,128)(2,1)} %get-tuple-element.274), channel_id=1, source_target_pairs={{0,2},{1,3},{2,0},{3,1},{4,6},{5,7},{6,4},{7,5},{8,10},{9,11},{10,... | collective-permute-start | bytes 3145736 | tf_op jit(solution)/shard_map/ppermute | solution.py:214
  784.6 42.5 %shard_map.104 = (bf16[64,32,256]{2,1,0:T(8,128)(2,1)}, bf16[64,32,256]{2,1,0:T(8,128)(2,1)}, bf16[64,32,256]{2,1,0:T(8,128)(2,1)}, bf16[64,32,256]{2,1,0:T(8,12...) custom-call(bf16[64,32,256]{2,1,0:T(8,128)(2,1)} %get-tuple-element., ...), custom_call_target="tpu_custom_call" | custom-call | flops 23622320128 | bytes 50331648 | tf_op jit(solution)/shard_map/pallas_call | solution.py:167
  828.5 26.4 %collective-permute-done.30.refs_11_ = bf16[64,32,256]{2,1,0:T(8,128)(2,1)} collective-permute-done((bf16[64,32,256]{2,1,0:T(8,128)(2,1)}, bf16[64,32,256]{2,1,0:T(8,128)(2,1)}, u32[]{:S(2)}, u32[]{:S(2)}) %collective-permute-start.30) | collective-permute-done | bytes 1048608 | tf_op jit(solution)/shard_map/ppermute | solution.py:214
  854.9 63.3 %collective-permute-done.32.refs_13_ = bf16[64,32,256]{2,1,0:T(8,128)(2,1)} collective-permute-done((bf16[64,32,256]{2,1,0:T(8,128)(2,1)S(1)}, bf16[64,32,256]{2,1,0:T(8,128)(2,1)}, u32[]{:S(2)}, u32[]{:S(2)}) %collective-permute-start.32) | collective-permute-done | bytes 1048608 | tf_op jit(solution)/shard_map/ppermute | solution.py:214
  918.3 22.7 %collective-permute-start.42 = (bf16[64,32,256]{2,1,0:T(8,128)(2,1)}, bf16[64,32,256]{2,1,0:T(8,128)(2,1)S(1)}, u32[]{:S(2)}, u32[]{:S(2)}) collective-permute-start(bf16[64,32,256]{2,1,0:T(8,128)(2,1)} %get-tuple-element.317), channel_id=1, source_target_pairs={{0,3},{1,2},{2,1},{3,0},{4,7},{5,6},{6,5},{7,4},{8,11},{9,10},{10,... | collective-permute-start | bytes 3145736 | tf_op jit(solution)/shard_map/ppermute | solution.py:214
  964.2 43.2 %shard_map.105 = (bf16[64,32,256]{2,1,0:T(8,128)(2,1)}, bf16[64,32,256]{2,1,0:T(8,128)(2,1)}, bf16[64,32,256]{2,1,0:T(8,128)(2,1)}, bf16[64,32,256]{2,1,0:T(8,12...) custom-call(bf16[64,32,256]{2,1,0:T(8,128)(2,1)} %get-tuple-element., ...), custom_call_target="tpu_custom_call" | custom-call | flops 23622320128 | bytes 50331648 | tf_op jit(solution)/shard_map/pallas_call | solution.py:167
  1010.4 42.7 %collective-permute-done.41.refs_0_ = bf16[64,32,256]{2,1,0:T(8,128)(2,1)} collective-permute-done((bf16[64,32,256]{2,1,0:T(8,128)(2,1)}, bf16[64,32,256]{2,1,0:T(8,128)(2,1)}, u32[]{:S(2)}, u32[]{:S(2)}) %collective-permute-start.41) | collective-permute-done | bytes 1048608 | tf_op jit(solution)/shard_map/ppermute | solution.py:214
  1087.6 61.0 %collective-permute-done.40.refs_1_ = bf16[64,32,256]{2,1,0:T(8,128)(2,1)S(1)} collective-permute-done((bf16[64,32,256]{2,1,0:T(8,128)(2,1)}, bf16[64,32,256]{2,1,0:T(8,128)(2,1)S(1)}, u32[]{:S(2)}, u32[]{:S(2)}) %collective-permute-start.40) | collective-permute-done | bytes 1048608 | tf_op jit(solution)/shard_map/ppermute | solution.py:214
  1174.5 51.3 %all-to-all-done = f32[32,16,256]{2,1,0:T(8,128)S(1)} async-done(((f32[32,16,256]{2,1,0:T(8,128)}), f32[32,16,256]{2,1,0:T(8,128)S(1)}, u32[]{:S(2)}, u32[]{:S(2)}) %all-to-all-start) | async-done | bytes 524320 | tf_op jit(solution)/shard_map/all_to_all | solution.py:273
  1239.0 27.7 %collective-permute-done.47.refs_1_ = bf16[64,32,256]{2,1,0:T(8,128)(2,1)} collective-permute-done((bf16[64,32,256]{2,1,0:T(8,128)(2,1)}, bf16[64,32,256]{2,1,0:T(8,128)(2,1)}, u32[]{:S(2)}, u32[]{:S(2)}) %collective-permute-start.47) | collective-permute-done | bytes 1048608 | tf_op jit(solution)/shard_map/ppermute | solution.py:214
  1279.9 53.2 %collective-permute-done.50.refs_0_ = bf16[64,32,256]{2,1,0:T(8,128)(2,1)S(1)} collective-permute-done((bf16[64,32,256]{2,1,0:T(8,128)(2,1)}, bf16[64,32,256]{2,1,0:T(8,128)(2,1)S(1)}, u32[]{:S(2)}, u32[]{:S(2)}) %collective-permute-start.50) | collective-permute-done | bytes 1048608 | tf_op jit(solution)/shard_map/ppermute | solution.py:214
  1360.4 27.9 %all-to-all-start.1 = ((f32[32,16,256]{2,1,0:T(8,128)}), f32[32,16,256]{2,1,0:T(8,128)S(1)}, u32[]{:S(2)}, u32[]{:S(2)}) async-start(f32[32,16,256]{2,1,0:T(8,128)} %broadcast_in_dim.3), calls=%async_computation.1 | async-start | bytes 1048576 | tf_op jit(solution)/shard_map/all_to_all | solution.py:294
  1407.1 23.7 %collective-permute-done.54.refs_1_ = bf16[64,32,256]{2,1,0:T(8,128)(2,1)} collective-permute-done((bf16[64,32,256]{2,1,0:T(8,128)(2,1)}, bf16[64,32,256]{2,1,0:T(8,128)(2,1)}, u32[]{:S(2)}, u32[]{:S(2)}) %collective-permute-start.54) | collective-permute-done | bytes 1048608 | tf_op jit(solution)/shard_map/ppermute | solution.py:214
  1450.9 31.7 %all-to-all-done.1 = f32[32,16,256]{2,1,0:T(8,128)S(1)} async-done(((f32[32,16,256]{2,1,0:T(8,128)}), f32[32,16,256]{2,1,0:T(8,128)S(1)}, u32[]{:S(2)}, u32[]{:S(2)}) %all-to-all-start.1) | async-done | bytes 524320 | tf_op jit(solution)/shard_map/all_to_all | solution.py:294
  (204 shorter events, 384.6 us)
Async XLA Ops:
  16.0 157.2 %collective-permute-start.4 = (bf16[64,32,256]{2,1,0:T(8,128)(2,1)}, bf16[64,32,256]{2,1,0:T(8,128)(2,1)}, u32[]{:S(2)}, u32[]{:S(2)}) collective-permute-start(bf16[64,32,256]{2,1,0:T(8,128)(2,1)} %get-tuple-element.196), channel_id=1, source_target_pairs={{0,4},{1,5},{2,6},{3,7},{4,0},{5,1},{6,2},{7,3},{8,12},{9,13},{10,... | collective-permute-start | bytes 3145736 | tf_op jit(solution)/shard_map/ppermute | solution.py:214
  19.5 153.9 %collective-permute-start = (bf16[64,32,256]{2,1,0:T(8,128)(2,1)}, bf16[64,32,256]{2,1,0:T(8,128)(2,1)}, u32[]{:S(2)}, u32[]{:S(2)}) collective-permute-start(bf16[64,32,256]{2,1,0:T(8,128)(2,1)} %get-tuple-element.186), channel_id=1, source_target_pairs={{0,6},{1,7},{2,4},{3,5},{4,2},{5,3},{6,0},{7,1},{8,14},{9,15},{10,... | collective-permute-start | bytes 3145736 | tf_op jit(solution)/shard_map/ppermute | solution.py:214
  47.2 143.5 %collective-permute-start.18 = (bf16[64,32,256]{2,1,0:T(8,128)(2,1)}, bf16[64,32,256]{2,1,0:T(8,128)(2,1)}, u32[]{:S(2)}, u32[]{:S(2)}) collective-permute-start(bf16[64,32,256]{2,1,0:T(8,128)(2,1)} %get-tuple-element.226), channel_id=1, source_target_pairs={{0,3},{1,2},{2,1},{3,0},{4,7},{5,6},{6,5},{7,4},{8,11},{9,10},{10,... | collective-permute-start | bytes 3145736 | tf_op jit(solution)/shard_map/ppermute | solution.py:214
  49.8 190.8 %collective-permute-start.23 = (bf16[64,32,256]{2,1,0:T(8,128)(2,1)}, bf16[64,32,256]{2,1,0:T(8,128)(2,1)}, u32[]{:S(2)}, u32[]{:S(2)}) collective-permute-start(bf16[64,32,256]{2,1,0:T(8,128)(2,1)} %get-tuple-element.237), channel_id=1, source_target_pairs={{0,4},{1,5},{2,6},{3,7},{4,0},{5,1},{6,2},{7,3},{8,12},{9,13},{10,... | collective-permute-start | bytes 3145736 | tf_op jit(solution)/shard_map/ppermute | solution.py:214
  105.6 179.9 %collective-permute-start.15 = (bf16[64,32,256]{2,1,0:T(8,128)(2,1)}, bf16[64,32,256]{2,1,0:T(8,128)(2,1)}, u32[]{:S(2)}, u32[]{:S(2)}) collective-permute-start(bf16[64,32,256]{2,1,0:T(8,128)(2,1)} %get-tuple-element.218), channel_id=1, source_target_pairs={{0,5},{1,4},{2,7},{3,6},{4,1},{5,0},{6,3},{7,2},{8,13},{9,12},{10,... | collective-permute-start | bytes 3145736 | tf_op jit(solution)/shard_map/ppermute | solution.py:214
  190.6 148.3 %collective-permute-start.1 = (bf16[64,32,256]{2,1,0:T(8,128)(2,1)}, bf16[64,32,256]{2,1,0:T(8,128)(2,1)S(1)}, u32[]{:S(2)}, u32[]{:S(2)}) collective-permute-start(bf16[64,32,256]{2,1,0:T(8,128)(2,1)} %get-tuple-element.187), channel_id=1, source_target_pairs={{0,2},{1,3},{2,0},{3,1},{4,6},{5,7},{6,4},{7,5},{8,10},{9,11},{10,... | collective-permute-start | bytes 3145736 | tf_op jit(solution)/shard_map/ppermute | solution.py:214
  288.7 135.2 %collective-permute-start.16 = (bf16[64,32,256]{2,1,0:T(8,128)(2,1)}, bf16[64,32,256]{2,1,0:T(8,128)(2,1)}, u32[]{:S(2)}, u32[]{:S(2)}) collective-permute-start(bf16[64,32,256]{2,1,0:T(8,128)(2,1)} %get-tuple-element.219), channel_id=1, source_target_pairs={{0,1},{1,0},{2,3},{3,2},{4,5},{5,4},{6,7},{7,6},{8,9},{9,8},{10,11... | collective-permute-start | bytes 3145736 | tf_op jit(solution)/shard_map/ppermute | solution.py:214
  288.9 156.3 %collective-permute-start.11 = (bf16[64,32,256]{2,1,0:T(8,128)(2,1)}, bf16[64,32,256]{2,1,0:T(8,128)(2,1)}, u32[]{:S(2)}, u32[]{:S(2)}) collective-permute-start(bf16[64,32,256]{2,1,0:T(8,128)(2,1)} %get-tuple-element.209), channel_id=1, source_target_pairs={{0,4},{1,5},{2,6},{3,7},{4,0},{5,1},{6,2},{7,3},{8,12},{9,13},{10,... | collective-permute-start | bytes 3145736 | tf_op jit(solution)/shard_map/ppermute | solution.py:214
  339.0 131.3 %collective-permute-start.2 = (bf16[64,32,256]{2,1,0:T(8,128)(2,1)}, bf16[64,32,256]{2,1,0:T(8,128)(2,1)}, u32[]{:S(2)}, u32[]{:S(2)}) collective-permute-start(bf16[64,32,256]{2,1,0:T(8,128)(2,1)} %get-tuple-element.188), channel_id=1, source_target_pairs={{0,5},{1,4},{2,7},{3,6},{4,1},{5,0},{6,3},{7,2},{8,13},{9,12},{10,... | collective-permute-start | bytes 3145736 | tf_op jit(solution)/shard_map/ppermute | solution.py:214
  423.8 157.0 %collective-permute-start.25 = (bf16[64,32,256]{2,1,0:T(8,128)(2,1)}, bf16[64,32,256]{2,1,0:T(8,128)(2,1)}, u32[]{:S(2)}, u32[]{:S(2)}) collective-permute-start(bf16[64,32,256]{2,1,0:T(8,128)(2,1)} %get-tuple-element.239), channel_id=1, source_target_pairs={{0,3},{1,2},{2,1},{3,0},{4,7},{5,6},{6,5},{7,4},{8,11},{9,10},{10,... | collective-permute-start | bytes 3145736 | tf_op jit(solution)/shard_map/ppermute | solution.py:214
  445.3 135.6 %collective-permute-start.17 = (bf16[64,32,256]{2,1,0:T(8,128)(2,1)}, bf16[64,32,256]{2,1,0:T(8,128)(2,1)S(1)}, u32[]{:S(2)}, u32[]{:S(2)}) collective-permute-start(bf16[64,32,256]{2,1,0:T(8,128)(2,1)} %get-tuple-element.220), channel_id=1, source_target_pairs={{0,4},{1,5},{2,6},{3,7},{4,0},{5,1},{6,2},{7,3},{8,12},{9,13},{10,... | collective-permute-start | bytes 3145736 | tf_op jit(solution)/shard_map/ppermute | solution.py:214
  455.7 137.0 %collective-permute-start.12 = (bf16[64,32,256]{2,1,0:T(8,128)(2,1)}, bf16[64,32,256]{2,1,0:T(8,128)(2,1)}, u32[]{:S(2)}, u32[]{:S(2)}) collective-permute-start(bf16[64,32,256]{2,1,0:T(8,128)(2,1)} %get-tuple-element.210), channel_id=1, source_target_pairs={{0,7},{1,6},{2,5},{3,4},{4,3},{5,2},{6,1},{7,0},{8,15},{9,14},{10,... | collective-permute-start | bytes 3145736 | tf_op jit(solution)/shard_map/ppermute | solution.py:214
  470.3 125.4 %collective-permute-start.7 = (bf16[64,32,256]{2,1,0:T(8,128)(2,1)}, bf16[64,32,256]{2,1,0:T(8,128)(2,1)}, u32[]{:S(2)}, u32[]{:S(2)}) collective-permute-start(bf16[64,32,256]{2,1,0:T(8,128)(2,1)} %get-tuple-element.199), channel_id=1, source_target_pairs={{0,6},{1,7},{2,4},{3,5},{4,2},{5,3},{6,0},{7,1},{8,14},{9,15},{10,... | collective-permute-start | bytes 3145736 | tf_op jit(solution)/shard_map/ppermute | solution.py:214
  496.4 174.9 %collective-permute-start.3 = (bf16[64,32,256]{2,1,0:T(8,128)(2,1)}, bf16[64,32,256]{2,1,0:T(8,128)(2,1)S(1)}, u32[]{:S(2)}, u32[]{:S(2)}) collective-permute-start(bf16[64,32,256]{2,1,0:T(8,128)(2,1)} %get-tuple-element.189), channel_id=1, source_target_pairs={{0,1},{1,0},{2,3},{3,2},{4,5},{5,4},{6,7},{7,6},{8,9},{9,8},{10,11... | collective-permute-start | bytes 3145736 | tf_op jit(solution)/shard_map/ppermute | solution.py:214
  595.6 165.6 %collective-permute-start.13 = (bf16[64,32,256]{2,1,0:T(8,128)(2,1)}, bf16[64,32,256]{2,1,0:T(8,128)(2,1)}, u32[]{:S(2)}, u32[]{:S(2)}) collective-permute-start(bf16[64,32,256]{2,1,0:T(8,128)(2,1)} %get-tuple-element.211), channel_id=1, source_target_pairs={{0,3},{1,2},{2,1},{3,0},{4,7},{5,6},{6,5},{7,4},{8,11},{9,10},{10,... | collective-permute-start | bytes 3145736 | tf_op jit(solution)/shard_map/ppermute | solution.py:214
  761.2 157.0 %collective-permute-start.33 = (bf16[64,32,256]{2,1,0:T(8,128)(2,1)}, bf16[64,32,256]{2,1,0:T(8,128)(2,1)}, u32[]{:S(2)}, u32[]{:S(2)}) collective-permute-start(bf16[64,32,256]{2,1,0:T(8,128)(2,1)} %get-tuple-element.286), channel_id=1, source_target_pairs={{0,6},{1,7},{2,4},{3,5},{4,2},{5,3},{6,0},{7,1},{8,14},{9,15},{10,... | collective-permute-start | bytes 3145736 | tf_op jit(solution)/shard_map/ppermute | solution.py:214
  782.5 135.8 %collective-permute-start.32 = (bf16[64,32,256]{2,1,0:T(8,128)(2,1)S(1)}, bf16[64,32,256]{2,1,0:T(8,128)(2,1)}, u32[]{:S(2)}, u32[]{:S(2)}) collective-permute-start(bf16[64,32,256]{2,1,0:T(8,128)(2,1)S(1)} %copy-done.19), channel_id=1, source_target_pairs={{0,5},{1,4},{2,7},{3,6},{4,1},{5,0},{6,3},{7,2},{8,13},{9,12},{10,... | collective-permute-start | bytes 3145736 | tf_op jit(solution)/shard_map/ppermute | solution.py:214
  782.7 135.6 %collective-permute-start.34 = (bf16[64,32,256]{2,1,0:T(8,128)(2,1)}, bf16[64,32,256]{2,1,0:T(8,128)(2,1)}, u32[]{:S(2)}, u32[]{:S(2)}) collective-permute-start(bf16[64,32,256]{2,1,0:T(8,128)(2,1)} %get-tuple-element.289), channel_id=1, source_target_pairs={{0,7},{1,6},{2,5},{3,4},{4,3},{5,2},{6,1},{7,0},{8,15},{9,14},{10,... | collective-permute-start | bytes 3145736 | tf_op jit(solution)/shard_map/ppermute | solution.py:214
  827.2 135.0 %collective-permute-start.35 = (bf16[64,32,256]{2,1,0:T(8,128)(2,1)}, bf16[64,32,256]{2,1,0:T(8,128)(2,1)S(1)}, u32[]{:S(2)}, u32[]{:S(2)}) collective-permute-start(bf16[64,32,256]{2,1,0:T(8,128)(2,1)} %get-tuple-element.295), channel_id=1, source_target_pairs={{0,4},{1,5},{2,6},{3,7},{4,0},{5,1},{6,2},{7,3},{8,12},{9,13},{10,... | collective-permute-start | bytes 3145736 | tf_op jit(solution)/shard_map/ppermute | solution.py:214
  942.2 143.2 %collective-permute-start.39 = (bf16[64,32,256]{2,1,0:T(8,128)(2,1)}, bf16[64,32,256]{2,1,0:T(8,128)(2,1)}, u32[]{:S(2)}, u32[]{:S(2)}) collective-permute-start(bf16[64,32,256]{2,1,0:T(8,128)(2,1)} %get-tuple-element.307), channel_id=1, source_target_pairs={{0,6},{1,7},{2,4},{3,5},{4,2},{5,3},{6,0},{7,1},{8,14},{9,15},{10,... | collective-permute-start | bytes 3145736 | tf_op jit(solution)/shard_map/ppermute | solution.py:214
  1010.3 138.3 %collective-permute-start.40 = (bf16[64,32,256]{2,1,0:T(8,128)(2,1)}, bf16[64,32,256]{2,1,0:T(8,128)(2,1)S(1)}, u32[]{:S(2)}, u32[]{:S(2)}) collective-permute-start(bf16[64,32,256]{2,1,0:T(8,128)(2,1)} %get-tuple-element.310), channel_id=1, source_target_pairs={{0,5},{1,4},{2,7},{3,6},{4,1},{5,0},{6,3},{7,2},{8,13},{9,12},{10,... | collective-permute-start | bytes 3145736 | tf_op jit(solution)/shard_map/ppermute | solution.py:214
  1053.1 172.7 %collective-permute-start.48 = (bf16[64,32,256]{2,1,0:T(8,128)(2,1)}, bf16[64,32,256]{2,1,0:T(8,128)(2,1)}, u32[]{:S(2)}, u32[]{:S(2)}) collective-permute-start(bf16[64,32,256]{2,1,0:T(8,128)(2,1)} %get-tuple-element.338), channel_id=1, source_target_pairs={{0,2},{1,3},{2,0},{3,1},{4,6},{5,7},{6,4},{7,5},{8,10},{9,11},{10,... | collective-permute-start | bytes 3145736 | tf_op jit(solution)/shard_map/ppermute | solution.py:214
  1076.7 149.1 %all-to-all-start = ((f32[32,16,256]{2,1,0:T(8,128)}), f32[32,16,256]{2,1,0:T(8,128)S(1)}, u32[]{:S(2)}, u32[]{:S(2)}) async-start(f32[32,16,256]{2,1,0:T(8,128)} %bitcast.6), calls=%async_computation | async-start | bytes 1048576 | tf_op jit(solution)/shard_map/all_to_all | solution.py:273
  1085.4 181.3 %collective-permute-start.47 = (bf16[64,32,256]{2,1,0:T(8,128)(2,1)}, bf16[64,32,256]{2,1,0:T(8,128)(2,1)}, u32[]{:S(2)}, u32[]{:S(2)}) collective-permute-start(bf16[64,32,256]{2,1,0:T(8,128)(2,1)} %get-tuple-element.335), channel_id=1, source_target_pairs={{0,5},{1,4},{2,7},{3,6},{4,1},{5,0},{6,3},{7,2},{8,13},{9,12},{10,... | collective-permute-start | bytes 3145736 | tf_op jit(solution)/shard_map/ppermute | solution.py:214
  (55 other events, 4759.1 us)

commit v3 on v1

--- a/solution.py
+++ b/solution.py
@@ -268,8 +268,10 @@
 
     def reduced():
         both = jnp.concatenate([first_sum, relative(relative(second_sum, 0), 1)])
-        shares = both.reshape(devices, -1, both.shape[1])
-        return jnp.sum(lax.all_to_all(shares, axes, 0, 0, tiled=True), axis=0)
+        for axis in axes:
+            shares = both.reshape(lax.axis_size(axis), -1, both.shape[1])
+            both = jnp.sum(lax.all_to_all(shares, axis, 0, 0, tiled=True), axis=0)
+        return both
 
     def early_grads():
         done = None

time: 1480 us -> 1480 us (level)
  waiting for transfers between devices: 824 us -> 802 us
  blocking collectives: 0 us -> 14.8 us
    all_to_all x1, waiting for transfers between devices: 51.3 us -> 0.01 us  [reduced(): both = jnp.sum(lax.all_to_all(shares, axis, 0, 0, tiled=True), axis=0)]
    ppermute x56, waiting for transfers between devices: 741 us -> 772 us  [__call__(): self.results.append(lax.ppermute(values, 'seq', pairs))]
  transfers between devices with their start and end apart: 58 -> 58, of which waited for: 26 -> 25; matrix products, arithmetic and copies ran while one was open for 0% -> 1% of each run, Pallas kernels for 15% -> 15%
where the time goes in v3:
time: 1480 us
  waiting for transfers between devices  802 us (54%)
  starting transfers between devices  427 us (29%)
  Pallas kernels  219 us (15%)
  blocking collectives  14.8 us (1%)
    ppermute x56, waiting for transfers between devices, __call__(): self.results.append(lax.ppermute(values, 'seq', pairs))  772 us
    ppermute x56, starting transfers between devices, __call__(): self.results.append(lax.ppermute(values, 'seq', pairs))  394 us
    pallas_call x2, Pallas kernels, mix(): pl.pallas_call(functools.partial(mix_kernel, parts, has_previous, is_last...  110 us
    pallas_call x20, Pallas kernels, leave(): pl.pallas_call(functools.partial(leave_kernel, group), grid_spec=pltpu.Pr...  70.5 us
    pallas_call x12, Pallas kernels, arrive(): pl.pallas_call(functools.partial(arrive_kernel, group), grid_spec=pltpu.P...  39.4 us
    all_to_all x1, waiting for transfers between devices, on_device(): lax.all_to_all(copies, axes, 0, 0, tiled=True).reshape(-1, block_size)  30.7 us
  transfers between devices with their start and end apart: 58, of which 25 were waited for; matrix products, arithmetic and copies ran while one was open for 1% of the time, Pallas kernels for 15%

profile of v3, /device:TPU:3, one launch (start us, length us, event | category | flops | bytes accessed | tf_op | source)
XLA Modules:
  0.0 1475.1 jit_solution(2027672493366486792)
XLA Ops:
  50.1 55.6 %collective-permute-done.9.refs_21_ = bf16[64,32,256]{2,1,0:T(8,128)(2,1)S(1)} collective-permute-done((bf16[64,32,256]{2,1,0:T(8,128)(2,1)}, bf16[64,32,256]{2,1,0:T(8,128)(2,1)S(1)}, u32[]{:S(2)}, u32[]{:S(2)}) %collective-permute-start.9) | collective-permute-done | bytes 1048608 | tf_op jit(solution)/shard_map/ppermute | solution.py:213
  105.6 67.5 %collective-permute-done.4.refs_20_ = bf16[64,32,256]{2,1,0:T(8,128)(2,1)} collective-permute-done((bf16[64,32,256]{2,1,0:T(8,128)(2,1)}, bf16[64,32,256]{2,1,0:T(8,128)(2,1)}, u32[]{:S(2)}, u32[]{:S(2)}) %collective-permute-start.4) | collective-permute-done | bytes 1048608 | tf_op jit(solution)/shard_map/ppermute | solution.py:213
  190.7 43.1 %collective-permute-start.1 = (bf16[64,32,256]{2,1,0:T(8,128)(2,1)}, bf16[64,32,256]{2,1,0:T(8,128)(2,1)S(1)}, u32[]{:S(2)}, u32[]{:S(2)}) collective-permute-start(bf16[64,32,256]{2,1,0:T(8,128)(2,1)} %get-tuple-element.187), channel_id=1, source_target_pairs={{0,2},{1,3},{2,0},{3,1},{4,6},{5,7},{6,4},{7,5},{8,10},{9,11},{10,... | collective-permute-start | bytes 3145736 | tf_op jit(solution)/shard_map/ppermute | solution.py:213
  242.8 42.7 %collective-permute-done.15.refs_5_ = bf16[64,32,256]{2,1,0:T(8,128)(2,1)} collective-permute-done((bf16[64,32,256]{2,1,0:T(8,128)(2,1)}, bf16[64,32,256]{2,1,0:T(8,128)(2,1)}, u32[]{:S(2)}, u32[]{:S(2)}) %collective-permute-start.15) | collective-permute-done | bytes 1048608 | tf_op jit(solution)/shard_map/ppermute | solution.py:213
  288.9 42.9 %collective-permute-start.11 = (bf16[64,32,256]{2,1,0:T(8,128)(2,1)}, bf16[64,32,256]{2,1,0:T(8,128)(2,1)}, u32[]{:S(2)}, u32[]{:S(2)}) collective-permute-start(bf16[64,32,256]{2,1,0:T(8,128)(2,1)} %get-tuple-element.209), channel_id=1, source_target_pairs={{0,4},{1,5},{2,6},{3,7},{4,0},{5,1},{6,2},{7,3},{8,12},{9,13},{10,... | collective-permute-start | bytes 3145736 | tf_op jit(solution)/shard_map/ppermute | solution.py:213
  339.0 37.8 %collective-permute-start.2 = (bf16[64,32,256]{2,1,0:T(8,128)(2,1)}, bf16[64,32,256]{2,1,0:T(8,128)(2,1)}, u32[]{:S(2)}, u32[]{:S(2)}) collective-permute-start(bf16[64,32,256]{2,1,0:T(8,128)(2,1)} %get-tuple-element.188), channel_id=1, source_target_pairs={{0,5},{1,4},{2,7},{3,6},{4,1},{5,0},{6,3},{7,2},{8,13},{9,12},{10,... | collective-permute-start | bytes 3145736 | tf_op jit(solution)/shard_map/ppermute | solution.py:213
  376.8 47.1 %collective-permute-start.20 = (bf16[64,32,256]{2,1,0:T(8,128)(2,1)}, bf16[64,32,256]{2,1,0:T(8,128)(2,1)}, u32[]{:S(2)}, u32[]{:S(2)}) collective-permute-start(bf16[64,32,256]{2,1,0:T(8,128)(2,1)} %get-tuple-element.228), channel_id=1, source_target_pairs={{0,2},{1,3},{2,0},{3,1},{4,6},{5,7},{6,4},{7,5},{8,10},{9,11},{10,... | collective-permute-start | bytes 3145736 | tf_op jit(solution)/shard_map/ppermute | solution.py:213
  470.3 26.1 %collective-permute-done.20.refs_10_ = bf16[64,32,256]{2,1,0:T(8,128)(2,1)} collective-permute-done((bf16[64,32,256]{2,1,0:T(8,128)(2,1)}, bf16[64,32,256]{2,1,0:T(8,128)(2,1)}, u32[]{:S(2)}, u32[]{:S(2)}) %collective-permute-start.20) | collective-permute-done | bytes 1048608 | tf_op jit(solution)/shard_map/ppermute | solution.py:213
  496.4 84.5 %collective-permute-done.25.refs_11_ = bf16[64,32,256]{2,1,0:T(8,128)(2,1)} collective-permute-done((bf16[64,32,256]{2,1,0:T(8,128)(2,1)}, bf16[64,32,256]{2,1,0:T(8,128)(2,1)}, u32[]{:S(2)}, u32[]{:S(2)}) %collective-permute-start.25) | collective-permute-done | bytes 1048608 | tf_op jit(solution)/shard_map/ppermute | solution.py:213
  595.7 75.5 %collective-permute-start.13 = (bf16[64,32,256]{2,1,0:T(8,128)(2,1)}, bf16[64,32,256]{2,1,0:T(8,128)(2,1)}, u32[]{:S(2)}, u32[]{:S(2)}) collective-permute-start(bf16[64,32,256]{2,1,0:T(8,128)(2,1)} %get-tuple-element.211), channel_id=1, source_target_pairs={{0,3},{1,2},{2,1},{3,0},{4,7},{5,6},{6,5},{7,4},{8,11},{9,10},{10,... | collective-permute-start | bytes 3145736 | tf_op jit(solution)/shard_map/ppermute | solution.py:213
  671.3 22.1 %collective-permute-done.21.refs_5_ = bf16[64,32,256]{2,1,0:T(8,128)(2,1)S(1)} collective-permute-done((bf16[64,32,256]{2,1,0:T(8,128)(2,1)}, bf16[64,32,256]{2,1,0:T(8,128)(2,1)S(1)}, u32[]{:S(2)}, u32[]{:S(2)}) %collective-permute-start.21) | collective-permute-done | bytes 1048608 | tf_op jit(solution)/shard_map/ppermute | solution.py:213
  703.6 57.6 %collective-permute-start.29 = (bf16[64,32,256]{2,1,0:T(8,128)(2,1)}, bf16[64,32,256]{2,1,0:T(8,128)(2,1)S(1)}, u32[]{:S(2)}, u32[]{:S(2)}) collective-permute-start(bf16[64,32,256]{2,1,0:T(8,128)(2,1)} %get-tuple-element.274), channel_id=1, source_target_pairs={{0,2},{1,3},{2,0},{3,1},{4,6},{5,7},{6,4},{7,5},{8,10},{9,11},{10,... | collective-permute-start | bytes 3145736 | tf_op jit(solution)/shard_map/ppermute | solution.py:213
  784.5 54.3 %shard_map.104 = (bf16[64,32,256]{2,1,0:T(8,128)(2,1)}, bf16[64,32,256]{2,1,0:T(8,128)(2,1)}, bf16[64,32,256]{2,1,0:T(8,128)(2,1)}, bf16[64,32,256]{2,1,0:T(8,12...) custom-call(bf16[64,32,256]{2,1,0:T(8,128)(2,1)} %get-tuple-element., ...), custom_call_target="tpu_custom_call" | custom-call | flops 23622320128 | bytes 50331648 | tf_op jit(solution)/shard_map/pallas_call | solution.py:166
  854.8 63.5 %collective-permute-done.32.refs_13_ = bf16[64,32,256]{2,1,0:T(8,128)(2,1)} collective-permute-done((bf16[64,32,256]{2,1,0:T(8,128)(2,1)}, bf16[64,32,256]{2,1,0:T(8,128)(2,1)}, u32[]{:S(2)}, u32[]{:S(2)}) %collective-permute-start.32) | collective-permute-done | bytes 1048608 | tf_op jit(solution)/shard_map/ppermute | solution.py:213
  918.3 22.7 %collective-permute-start.42 = (bf16[64,32,256]{2,1,0:T(8,128)(2,1)}, bf16[64,32,256]{2,1,0:T(8,128)(2,1)S(1)}, u32[]{:S(2)}, u32[]{:S(2)}) collective-permute-start(bf16[64,32,256]{2,1,0:T(8,128)(2,1)} %get-tuple-element.317), channel_id=1, source_target_pairs={{0,3},{1,2},{2,1},{3,0},{4,7},{5,6},{6,5},{7,4},{8,11},{9,10},{10,... | collective-permute-start | bytes 3145736 | tf_op jit(solution)/shard_map/ppermute | solution.py:213
  964.2 55.3 %shard_map.105 = (bf16[64,32,256]{2,1,0:T(8,128)(2,1)}, bf16[64,32,256]{2,1,0:T(8,128)(2,1)}, bf16[64,32,256]{2,1,0:T(8,128)(2,1)}, bf16[64,32,256]{2,1,0:T(8,12...) custom-call(bf16[64,32,256]{2,1,0:T(8,128)(2,1)} %get-tuple-element., ...), custom_call_target="tpu_custom_call" | custom-call | flops 23622320128 | bytes 50331648 | tf_op jit(solution)/shard_map/pallas_call | solution.py:166
  1020.8 32.3 %collective-permute-done.41.refs_0_ = bf16[64,32,256]{2,1,0:T(8,128)(2,1)S(1)} collective-permute-done((bf16[64,32,256]{2,1,0:T(8,128)(2,1)}, bf16[64,32,256]{2,1,0:T(8,128)(2,1)S(1)}, u32[]{:S(2)}, u32[]{:S(2)}) %collective-permute-start.41) | collective-permute-done | bytes 1048608 | tf_op jit(solution)/shard_map/ppermute | solution.py:213
  1053.3 22.5 %collective-permute-start.45 = (bf16[64,32,256]{2,1,0:T(8,128)(2,1)}, bf16[64,32,256]{2,1,0:T(8,128)(2,1)}, u32[]{:S(2)}, u32[]{:S(2)}) collective-permute-start(bf16[64,32,256]{2,1,0:T(8,128)(2,1)} %get-tuple-element.330), channel_id=1, source_target_pairs={{0,4},{1,5},{2,6},{3,7},{4,0},{5,1},{6,2},{7,3},{8,12},{9,13},{10,... | collective-permute-start | bytes 3145736 | tf_op jit(solution)/shard_map/ppermute | solution.py:213
  1101.5 42.9 %collective-permute-done.40.refs_1_ = bf16[64,32,256]{2,1,0:T(8,128)(2,1)S(1)} collective-permute-done((bf16[64,32,256]{2,1,0:T(8,128)(2,1)}, bf16[64,32,256]{2,1,0:T(8,128)(2,1)S(1)}, u32[]{:S(2)}, u32[]{:S(2)}) %collective-permute-start.40) | collective-permute-done | bytes 1048608 | tf_op jit(solution)/shard_map/ppermute | solution.py:213
  1183.5 74.8 %collective-permute-done.47.refs_1_ = bf16[64,32,256]{2,1,0:T(8,128)(2,1)} collective-permute-done((bf16[64,32,256]{2,1,0:T(8,128)(2,1)}, bf16[64,32,256]{2,1,0:T(8,128)(2,1)}, u32[]{:S(2)}, u32[]{:S(2)}) %collective-permute-start.47) | collective-permute-done | bytes 1048608 | tf_op jit(solution)/shard_map/ppermute | solution.py:213
  1271.5 53.3 %collective-permute-done.50.refs_0_ = bf16[64,32,256]{2,1,0:T(8,128)(2,1)} collective-permute-done((bf16[64,32,256]{2,1,0:T(8,128)(2,1)}, bf16[64,32,256]{2,1,0:T(8,128)(2,1)}, u32[]{:S(2)}, u32[]{:S(2)}) %collective-permute-start.50) | collective-permute-done | bytes 1048608 | tf_op jit(solution)/shard_map/ppermute | solution.py:213
  1352.1 27.8 %all-to-all-start.2 = ((f32[32,16,256]{2,1,0:T(8,128)}), f32[32,16,256]{2,1,0:T(8,128)S(1)}, u32[]{:S(2)}, u32[]{:S(2)}) async-start(f32[32,16,256]{2,1,0:T(8,128)} %broadcast_in_dim.3), calls=%async_computation.2 | async-start | bytes 1048576 | tf_op jit(solution)/shard_map/all_to_all | solution.py:295
  1398.8 23.8 %collective-permute-done.54.refs_1_ = bf16[64,32,256]{2,1,0:T(8,128)(2,1)} collective-permute-done((bf16[64,32,256]{2,1,0:T(8,128)(2,1)}, bf16[64,32,256]{2,1,0:T(8,128)(2,1)}, u32[]{:S(2)}, u32[]{:S(2)}) %collective-permute-start.54) | collective-permute-done | bytes 1048608 | tf_op jit(solution)/shard_map/ppermute | solution.py:213
  1443.5 30.7 %all-to-all-done.2 = f32[32,16,256]{2,1,0:T(8,128)S(1)} async-done(((f32[32,16,256]{2,1,0:T(8,128)}), f32[32,16,256]{2,1,0:T(8,128)S(1)}, u32[]{:S(2)}, u32[]{:S(2)}) %all-to-all-start.2) | async-done | bytes 524320 | tf_op jit(solution)/shard_map/all_to_all | solution.py:295
  (210 shorter events, 367.8 us)
Async XLA Ops:
  16.0 157.2 %collective-permute-start.4 = (bf16[64,32,256]{2,1,0:T(8,128)(2,1)}, bf16[64,32,256]{2,1,0:T(8,128)(2,1)}, u32[]{:S(2)}, u32[]{:S(2)}) collective-permute-start(bf16[64,32,256]{2,1,0:T(8,128)(2,1)} %get-tuple-element.196), channel_id=1, source_target_pairs={{0,4},{1,5},{2,6},{3,7},{4,0},{5,1},{6,2},{7,3},{8,12},{9,13},{10,... | collective-permute-start | bytes 3145736 | tf_op jit(solution)/shard_map/ppermute | solution.py:213
  19.5 153.9 %collective-permute-start = (bf16[64,32,256]{2,1,0:T(8,128)(2,1)}, bf16[64,32,256]{2,1,0:T(8,128)(2,1)}, u32[]{:S(2)}, u32[]{:S(2)}) collective-permute-start(bf16[64,32,256]{2,1,0:T(8,128)(2,1)} %get-tuple-element.186), channel_id=1, source_target_pairs={{0,6},{1,7},{2,4},{3,5},{4,2},{5,3},{6,0},{7,1},{8,14},{9,15},{10,... | collective-permute-start | bytes 3145736 | tf_op jit(solution)/shard_map/ppermute | solution.py:213
  47.2 143.5 %collective-permute-start.18 = (bf16[64,32,256]{2,1,0:T(8,128)(2,1)}, bf16[64,32,256]{2,1,0:T(8,128)(2,1)}, u32[]{:S(2)}, u32[]{:S(2)}) collective-permute-start(bf16[64,32,256]{2,1,0:T(8,128)(2,1)} %get-tuple-element.226), channel_id=1, source_target_pairs={{0,3},{1,2},{2,1},{3,0},{4,7},{5,6},{6,5},{7,4},{8,11},{9,10},{10,... | collective-permute-start | bytes 3145736 | tf_op jit(solution)/shard_map/ppermute | solution.py:213
  49.8 190.8 %collective-permute-start.23 = (bf16[64,32,256]{2,1,0:T(8,128)(2,1)}, bf16[64,32,256]{2,1,0:T(8,128)(2,1)}, u32[]{:S(2)}, u32[]{:S(2)}) collective-permute-start(bf16[64,32,256]{2,1,0:T(8,128)(2,1)} %get-tuple-element.237), channel_id=1, source_target_pairs={{0,4},{1,5},{2,6},{3,7},{4,0},{5,1},{6,2},{7,3},{8,12},{9,13},{10,... | collective-permute-start | bytes 3145736 | tf_op jit(solution)/shard_map/ppermute | solution.py:213
  105.6 179.9 %collective-permute-start.15 = (bf16[64,32,256]{2,1,0:T(8,128)(2,1)}, bf16[64,32,256]{2,1,0:T(8,128)(2,1)}, u32[]{:S(2)}, u32[]{:S(2)}) collective-permute-start(bf16[64,32,256]{2,1,0:T(8,128)(2,1)} %get-tuple-element.218), channel_id=1, source_target_pairs={{0,5},{1,4},{2,7},{3,6},{4,1},{5,0},{6,3},{7,2},{8,13},{9,12},{10,... | collective-permute-start | bytes 3145736 | tf_op jit(solution)/shard_map/ppermute | solution.py:213
  190.7 148.2 %collective-permute-start.1 = (bf16[64,32,256]{2,1,0:T(8,128)(2,1)}, bf16[64,32,256]{2,1,0:T(8,128)(2,1)S(1)}, u32[]{:S(2)}, u32[]{:S(2)}) collective-permute-start(bf16[64,32,256]{2,1,0:T(8,128)(2,1)} %get-tuple-element.187), channel_id=1, source_target_pairs={{0,2},{1,3},{2,0},{3,1},{4,6},{5,7},{6,4},{7,5},{8,10},{9,11},{10,... | collective-permute-start | bytes 3145736 | tf_op jit(solution)/shard_map/ppermute | solution.py:213
  288.7 135.2 %collective-permute-start.16 = (bf16[64,32,256]{2,1,0:T(8,128)(2,1)}, bf16[64,32,256]{2,1,0:T(8,128)(2,1)}, u32[]{:S(2)}, u32[]{:S(2)}) collective-permute-start(bf16[64,32,256]{2,1,0:T(8,128)(2,1)} %get-tuple-element.219), channel_id=1, source_target_pairs={{0,1},{1,0},{2,3},{3,2},{4,5},{5,4},{6,7},{7,6},{8,9},{9,8},{10,11... | collective-permute-start | bytes 3145736 | tf_op jit(solution)/shard_map/ppermute | solution.py:213
  288.9 156.3 %collective-permute-start.11 = (bf16[64,32,256]{2,1,0:T(8,128)(2,1)}, bf16[64,32,256]{2,1,0:T(8,128)(2,1)}, u32[]{:S(2)}, u32[]{:S(2)}) collective-permute-start(bf16[64,32,256]{2,1,0:T(8,128)(2,1)} %get-tuple-element.209), channel_id=1, source_target_pairs={{0,4},{1,5},{2,6},{3,7},{4,0},{5,1},{6,2},{7,3},{8,12},{9,13},{10,... | collective-permute-start | bytes 3145736 | tf_op jit(solution)/shard_map/ppermute | solution.py:213
  339.0 131.3 %collective-permute-start.2 = (bf16[64,32,256]{2,1,0:T(8,128)(2,1)}, bf16[64,32,256]{2,1,0:T(8,128)(2,1)}, u32[]{:S(2)}, u32[]{:S(2)}) collective-permute-start(bf16[64,32,256]{2,1,0:T(8,128)(2,1)} %get-tuple-element.188), channel_id=1, source_target_pairs={{0,5},{1,4},{2,7},{3,6},{4,1},{5,0},{6,3},{7,2},{8,13},{9,12},{10,... | collective-permute-start | bytes 3145736 | tf_op jit(solution)/shard_map/ppermute | solution.py:213
  423.8 157.0 %collective-permute-start.25 = (bf16[64,32,256]{2,1,0:T(8,128)(2,1)}, bf16[64,32,256]{2,1,0:T(8,128)(2,1)}, u32[]{:S(2)}, u32[]{:S(2)}) collective-permute-start(bf16[64,32,256]{2,1,0:T(8,128)(2,1)} %get-tuple-element.239), channel_id=1, source_target_pairs={{0,3},{1,2},{2,1},{3,0},{4,7},{5,6},{6,5},{7,4},{8,11},{9,10},{10,... | collective-permute-start | bytes 3145736 | tf_op jit(solution)/shard_map/ppermute | solution.py:213
  445.3 135.6 %collective-permute-start.17 = (bf16[64,32,256]{2,1,0:T(8,128)(2,1)}, bf16[64,32,256]{2,1,0:T(8,128)(2,1)S(1)}, u32[]{:S(2)}, u32[]{:S(2)}) collective-permute-start(bf16[64,32,256]{2,1,0:T(8,128)(2,1)} %get-tuple-element.220), channel_id=1, source_target_pairs={{0,4},{1,5},{2,6},{3,7},{4,0},{5,1},{6,2},{7,3},{8,12},{9,13},{10,... | collective-permute-start | bytes 3145736 | tf_op jit(solution)/shard_map/ppermute | solution.py:213
  455.8 137.0 %collective-permute-start.12 = (bf16[64,32,256]{2,1,0:T(8,128)(2,1)}, bf16[64,32,256]{2,1,0:T(8,128)(2,1)}, u32[]{:S(2)}, u32[]{:S(2)}) collective-permute-start(bf16[64,32,256]{2,1,0:T(8,128)(2,1)} %get-tuple-element.210), channel_id=1, source_target_pairs={{0,7},{1,6},{2,5},{3,4},{4,3},{5,2},{6,1},{7,0},{8,15},{9,14},{10,... | collective-permute-start | bytes 3145736 | tf_op jit(solution)/shard_map/ppermute | solution.py:213
  470.3 125.5 %collective-permute-start.7 = (bf16[64,32,256]{2,1,0:T(8,128)(2,1)}, bf16[64,32,256]{2,1,0:T(8,128)(2,1)}, u32[]{:S(2)}, u32[]{:S(2)}) collective-permute-start(bf16[64,32,256]{2,1,0:T(8,128)(2,1)} %get-tuple-element.199), channel_id=1, source_target_pairs={{0,6},{1,7},{2,4},{3,5},{4,2},{5,3},{6,0},{7,1},{8,14},{9,15},{10,... | collective-permute-start | bytes 3145736 | tf_op jit(solution)/shard_map/ppermute | solution.py:213
  496.4 174.9 %collective-permute-start.3 = (bf16[64,32,256]{2,1,0:T(8,128)(2,1)}, bf16[64,32,256]{2,1,0:T(8,128)(2,1)S(1)}, u32[]{:S(2)}, u32[]{:S(2)}) collective-permute-start(bf16[64,32,256]{2,1,0:T(8,128)(2,1)} %get-tuple-element.189), channel_id=1, source_target_pairs={{0,1},{1,0},{2,3},{3,2},{4,5},{5,4},{6,7},{7,6},{8,9},{9,8},{10,11... | collective-permute-start | bytes 3145736 | tf_op jit(solution)/shard_map/ppermute | solution.py:213
  595.7 165.5 %collective-permute-start.13 = (bf16[64,32,256]{2,1,0:T(8,128)(2,1)}, bf16[64,32,256]{2,1,0:T(8,128)(2,1)}, u32[]{:S(2)}, u32[]{:S(2)}) collective-permute-start(bf16[64,32,256]{2,1,0:T(8,128)(2,1)} %get-tuple-element.211), channel_id=1, source_target_pairs={{0,3},{1,2},{2,1},{3,0},{4,7},{5,6},{6,5},{7,4},{8,11},{9,10},{10,... | collective-permute-start | bytes 3145736 | tf_op jit(solution)/shard_map/ppermute | solution.py:213
  703.6 135.2 %collective-permute-start.29 = (bf16[64,32,256]{2,1,0:T(8,128)(2,1)}, bf16[64,32,256]{2,1,0:T(8,128)(2,1)S(1)}, u32[]{:S(2)}, u32[]{:S(2)}) collective-permute-start(bf16[64,32,256]{2,1,0:T(8,128)(2,1)} %get-tuple-element.274), channel_id=1, source_target_pairs={{0,2},{1,3},{2,0},{3,1},{4,6},{5,7},{6,4},{7,5},{8,10},{9,11},{10,... | collective-permute-start | bytes 3145736 | tf_op jit(solution)/shard_map/ppermute | solution.py:213
  761.2 157.0 %collective-permute-start.33 = (bf16[64,32,256]{2,1,0:T(8,128)(2,1)}, bf16[64,32,256]{2,1,0:T(8,128)(2,1)}, u32[]{:S(2)}, u32[]{:S(2)}) collective-permute-start(bf16[64,32,256]{2,1,0:T(8,128)(2,1)} %get-tuple-element.286), channel_id=1, source_target_pairs={{0,6},{1,7},{2,4},{3,5},{4,2},{5,3},{6,0},{7,1},{8,14},{9,15},{10,... | collective-permute-start | bytes 3145736 | tf_op jit(solution)/shard_map/ppermute | solution.py:213
  782.5 135.8 %collective-permute-start.32 = (bf16[64,32,256]{2,1,0:T(8,128)(2,1)}, bf16[64,32,256]{2,1,0:T(8,128)(2,1)}, u32[]{:S(2)}, u32[]{:S(2)}) collective-permute-start(bf16[64,32,256]{2,1,0:T(8,128)(2,1)} %get-tuple-element.283), channel_id=1, source_target_pairs={{0,5},{1,4},{2,7},{3,6},{4,1},{5,0},{6,3},{7,2},{8,13},{9,12},{10,... | collective-permute-start | bytes 3145736 | tf_op jit(solution)/shard_map/ppermute | solution.py:213
  782.7 135.6 %collective-permute-start.34 = (bf16[64,32,256]{2,1,0:T(8,128)(2,1)}, bf16[64,32,256]{2,1,0:T(8,128)(2,1)}, u32[]{:S(2)}, u32[]{:S(2)}) collective-permute-start(bf16[64,32,256]{2,1,0:T(8,128)(2,1)} %get-tuple-element.289), channel_id=1, source_target_pairs={{0,7},{1,6},{2,5},{3,4},{4,3},{5,2},{6,1},{7,0},{8,15},{9,14},{10,... | collective-permute-start | bytes 3145736 | tf_op jit(solution)/shard_map/ppermute | solution.py:213
  838.8 123.4 %collective-permute-start.35 = (bf16[64,32,256]{2,1,0:T(8,128)(2,1)}, bf16[64,32,256]{2,1,0:T(8,128)(2,1)S(1)}, u32[]{:S(2)}, u32[]{:S(2)}) collective-permute-start(bf16[64,32,256]{2,1,0:T(8,128)(2,1)} %get-tuple-element.295), channel_id=1, source_target_pairs={{0,4},{1,5},{2,6},{3,7},{4,0},{5,1},{6,2},{7,3},{8,12},{9,13},{10,... | collective-permute-start | bytes 3145736 | tf_op jit(solution)/shard_map/ppermute | solution.py:213
  942.2 157.2 %collective-permute-start.39 = (bf16[64,32,256]{2,1,0:T(8,128)(2,1)}, bf16[64,32,256]{2,1,0:T(8,128)(2,1)}, u32[]{:S(2)}, u32[]{:S(2)}) collective-permute-start(bf16[64,32,256]{2,1,0:T(8,128)(2,1)} %get-tuple-element.307), channel_id=1, source_target_pairs={{0,6},{1,7},{2,4},{3,5},{4,2},{5,3},{6,0},{7,1},{8,14},{9,15},{10,... | collective-permute-start | bytes 3145736 | tf_op jit(solution)/shard_map/ppermute | solution.py:213
  1020.7 123.8 %collective-permute-start.40 = (bf16[64,32,256]{2,1,0:T(8,128)(2,1)}, bf16[64,32,256]{2,1,0:T(8,128)(2,1)S(1)}, u32[]{:S(2)}, u32[]{:S(2)}) collective-permute-start(bf16[64,32,256]{2,1,0:T(8,128)(2,1)} %get-tuple-element.310), channel_id=1, source_target_pairs={{0,5},{1,4},{2,7},{3,6},{4,1},{5,0},{6,3},{7,2},{8,13},{9,12},{10,... | collective-permute-start | bytes 3145736 | tf_op jit(solution)/shard_map/ppermute | solution.py:213
  1099.4 158.9 %collective-permute-start.47 = (bf16[64,32,256]{2,1,0:T(8,128)(2,1)}, bf16[64,32,256]{2,1,0:T(8,128)(2,1)}, u32[]{:S(2)}, u32[]{:S(2)}) collective-permute-start(bf16[64,32,256]{2,1,0:T(8,128)(2,1)} %get-tuple-element.335), channel_id=1, source_target_pairs={{0,5},{1,4},{2,7},{3,6},{4,1},{5,0},{6,3},{7,2},{8,13},{9,12},{10,... | collective-permute-start | bytes 3145736 | tf_op jit(solution)/shard_map/ppermute | solution.py:213
  1170.3 154.5 %collective-permute-start.50 = (bf16[64,32,256]{2,1,0:T(8,128)(2,1)}, bf16[64,32,256]{2,1,0:T(8,128)(2,1)}, u32[]{:S(2)}, u32[]{:S(2)}) collective-permute-start(bf16[64,32,256]{2,1,0:T(8,128)(2,1)} %get-tuple-element.346), channel_id=1, source_target_pairs={{0,4},{1,5},{2,6},{3,7},{4,0},{5,1},{6,2},{7,3},{8,12},{9,13},{10,... | collective-permute-start | bytes 3145736 | tf_op jit(solution)/shard_map/ppermute | solution.py:213
  (57 other events, 4697.3 us)
